TPU v7x, 32 devices: a whole 2x2x4 slice. The times are simulated.
32 devices in a mesh: seg: 8 (over z, x), rep: 4 (over y, core).
Axes of the slice: x: 2, y: 2, z: 4, core: 2. Of those that a mesh axis runs over, the one named last changes fastest.
Arguments:
- layer_input: bfloat16 [4, 1536, 1024], P('rep', 'seg'), may hold values from -6 to 6
- live: int32 [4, 1536], P('rep', 'seg'), may hold values from 0 to 1, as said below
- knn_index: int32 [4, 1536, 128], P('rep', 'seg'), may hold values from -1 to 2879, as said below
- mem_keys: bfloat16 [4, 1536, 1024], P('rep', 'seg'), may hold values from -6 to 6
- mem_values: bfloat16 [4, 1536, 1024], P('rep', 'seg'), may hold values from -6 to 6
- gain_attn: bfloat16 [1024], P(('seg', 'rep')), may hold values from 0.099609375 to 1.8984375
- w_query: bfloat16 [1024, 1024], P(('seg', 'rep')), may hold values from -0.1875 to 0.1875
- w_key: bfloat16 [1024, 1024], P(('seg', 'rep')), may hold values from -0.1875 to 0.1875
- w_value: bfloat16 [1024, 1024], P(('seg', 'rep')), may hold values from -0.1875 to 0.1875
- w_out: bfloat16 [1024, 1024], P(('seg', 'rep')), may hold values from -2 to 2
- gain_ffn: bfloat16 [1024], P(('seg', 'rep')), may hold values from 0.099609375 to 1.8984375
- w_gate: bfloat16 [1024, 2816], P(('seg', 'rep')), may hold values from -0.1875 to 0.1875
- w_up: bfloat16 [1024, 2816], P(('seg', 'rep')), may hold values from -0.1875 to 0.1875
- w_down: bfloat16 [2816, 1024], P(('seg', 'rep')), may hold values from -0.109375 to 0.109375
- cotangent: bfloat16 [4, 1536, 1024], P('rep', 'seg'), may hold values from -6 to 6
Outputs:
- layer_output: bfloat16 [4, 1536, 1024], P('rep', 'seg')
- grad_x: bfloat16 [4, 1536, 1024], P('rep', 'seg')
- grad_gain_attn: float32 [1024], P(('seg', 'rep'))
- grad_w_query: float32 [1024, 1024], P(('seg', 'rep'))
- grad_w_key: float32 [1024, 1024], P(('seg', 'rep'))
- grad_w_value: float32 [1024, 1024], P(('seg', 'rep'))
- grad_w_out: float32 [1024, 1024], P(('seg', 'rep'))
- grad_gain_ffn: float32 [1024], P(('seg', 'rep'))
- grad_w_gate: float32 [1024, 2816], P(('seg', 'rep'))
- grad_w_up: float32 [1024, 2816], P(('seg', 'rep'))
- grad_w_down: float32 [2816, 1024], P(('seg', 'rep'))
Inputs may be any that keep to these rules, and one draw needn't show every extreme that they name: `knn_index`: each pick is a live slot of the query's row (m) or of the paired row (1536 + m) that lies in an earlier segment than the query's own; -1 marks an empty pick; a slot may repeat and counts once; queries of a row's first segment retrieve nothing. Padded slots fill the tail of a document's last segment; the first token of every segment is live; in every draw some pair of rows each hold one document over all their segments.
All inputs are finite; a program needn't handle non-finite values.
Results may differ from a plain program's by a relative error of at most 0.023.
Values may be sent and summed in bfloat16 or wider, within the bound.
No kernel may reach another device: no remote copies, remote signals or barrier semaphores. Data moves between devices by JAX's collectives and lax.ppermute only.
A program may use at most 320 MiB of HBM per device.

v0:
```python
import jax
import jax.numpy as jnp
from jax import lax
from jax.experimental import pallas as pl
from jax.experimental.pallas import tpu as pltpu
from jax.sharding import PartitionSpec as P

H = 8
HD = 128
EPSILON = 1e-05
NEG_BIG = -1e30
POS_BIG = 1e30
ROPE_BASE = 10000.0
LANES = 128
KERNEL_HIGH = 2
VMEM_BYTES = 44 * 1024 * 1024

SHORT = pl.CostEstimate(flops=1000, bytes_accessed=1000, transcendentals=0)

BF = jnp.bfloat16
F32 = jnp.float32


def cdiv(a, b):
    return -(-a // b)


def flip(value, axis, bit):
    count = lax.axis_size(axis)
    return lax.ppermute(value, axis, [(i, i ^ bit) for i in range(count)])


def flip_core(value):
    return flip(value, "rep", 1)


def flip_y(value):
    return flip(value, "rep", 2)


def flip_x(value):
    return flip(value, "seg", 1)


def flip_z(value):
    return flip(value, "seg", 2)


def ordered(mine, other, bit, axis):
    first = jnp.where(bit == 0, mine, other)
    second = jnp.where(bit == 0, other, mine)
    return jnp.concatenate([first, second], axis)


def pick(value, index, axis):
    return lax.dynamic_index_in_dim(value, index, axis, keepdims=False)


def cut(value, start, size, axis=-1):
    return lax.dynamic_slice_in_dim(value, start, size, axis % value.ndim)


def fence(*values):
    return lax.optimization_barrier(values)


def place():
    seg = lax.axis_index("seg")
    rep = lax.axis_index("rep")
    return seg % 2, (seg // 2) % 2, seg // 4, rep // 2, rep % 2


def high_bits():
    bit = 4
    out = []
    while bit < lax.axis_size("seg"):
        out.append(bit)
        bit *= 2
    return out


def gather_high(cur):
    seg = lax.axis_index("seg")
    for bit in high_bits():
        cur = ordered(cur, flip(cur, "seg", bit), (seg // bit) % 2, 0)
    return cur


def gather_x(cur):
    return ordered(cur, flip_x(cur), place()[0], 2)


def gather_y(cur):
    return ordered(cur, flip_y(cur), place()[3], 3)


def gather_high_pair(cur):
    seg = lax.axis_index("seg")
    cur = cur[:, None]
    bits = high_bits()
    for bit in bits[:-1]:
        cur = ordered(cur, flip(cur, "seg", bit), (seg // bit) % 2, 1)
    recv = flip(cur, "seg", bits[-1])
    side = (seg // bits[-1]) % 2
    return [ordered(cur[i], recv[i], side, 0)[:, :, None, None] for i in range(2)]


def flat(cur):
    return cur.reshape(-1, cur.shape[-1])


def halve(value, axis_name, bit, side, axis):
    recv = flip(pick(value, 1 - side, axis), axis_name, bit)
    kept = pick(value, side, axis)
    return (kept.astype(F32) + recv.astype(F32)).astype(BF)


def plane_shape(value, low):
    high = lax.axis_size("seg") // 4
    return value.reshape(high, low, 2, -1, value.shape[-1])


def halves(cur, axis, side):
    return pick(cur, side, axis), pick(cur, 1 - side, axis)


def plane_flips(parts):
    n_rep = lax.axis_size("rep")
    count = lax.axis_size("seg") * n_rep
    far = [(i, i ^ n_rep ^ 2) for i in range(count)]
    return flip_x(parts[0]), flip_y(parts[1]), lax.ppermute(parts[2], ("seg", "rep"), far)


def add_all(first, *others):
    total = first.astype(F32)
    for other in others:
        total = total + other.astype(F32)
    return total.astype(BF)


def z_flips(parts):
    return flip_z(parts[1]), flip(parts[2], "seg", 4), flip(parts[3], "seg", 6)


def z_plain(cur):
    low = place()[1]
    sums = reduce_high(cur)
    return ordered(pick(sums, low, 0)[None], flip_z(pick(sums, 1 - low, 0))[None], low, 0)


def reduce_high(cur):
    seg = lax.axis_index("seg")
    for bit in reversed(high_bits()):
        cur = cur.reshape((2, cur.shape[0] // 2) + cur.shape[1:])
        cur = halve(cur, "seg", bit, (seg // bit) % 2, 0)
    return cur[0]


def trade_core(quarters):
    core = place()[4]
    low, unused, rows, cols = 2, 2, quarters.shape[1], quarters.shape[2]
    four = quarters.reshape(2, 2, rows, cols)
    return ordered(pick(four, core, 1), flip_core(pick(four, 1 - core, 1)), core, 1)


def trade_z(halves):
    low = place()[1]
    return ordered(pick(halves, low, 0)[None], flip_z(pick(halves, 1 - low, 0))[None], low, 0)


def gather_z_four(halves):
    seg = lax.axis_index("seg")
    low = (seg // 2) % 2
    keep, give = pick(halves, low, 0)[None, None], pick(halves, 1 - low, 0)[None, None]
    near = ordered(keep, flip(give, "seg", 2), low, 1)
    far = ordered(flip(keep, "seg", 4), flip(give, "seg", 6), low, 1)
    return ordered(near, far, (seg // 4) % 2, 0)[:, :, None, None]


def start_gather(traded):
    return traded[None, :, None, None]


def core_halves(mine):
    core = place()[4]
    four = mine.reshape(2, 2, mine.shape[1] // 2, mine.shape[2])
    return halves(four, 1, core)


def all_blocks(by_low):
    both = jnp.stack([by_low, flip_core(by_low)], 1)
    return both.reshape((-1,) + by_low.shape[1:])


def two_rows(value):
    return ordered(value[None], flip_z(value)[None], place()[1], 0)


def core_parts(part):
    blocks = part.reshape((2, 2, part.shape[0] // 4) + part.shape[1:])
    return blocks[:, 0].astype(BF), blocks[:, 1].astype(BF)


def core_sums(part):
    blocks = part.reshape((2, 2, part.shape[0] // 4) + part.shape[1:])
    return (blocks[:, 0] + flip_core(blocks[:, 1].astype(BF)).astype(F32)).astype(BF)


def own_sums(sums):
    low = place()[1]
    return pick(sums, low, 0).astype(F32) + flip_z(pick(sums, 1 - low, 0)).astype(F32)


def z_sums(sums):
    return (sums.astype(F32) + flip_z(sums).astype(F32)).astype(BF)


def both_cores(sums):
    return jnp.stack([sums, flip_core(sums)], 1).astype(F32)


def unit_blocks(n_blocks):
    order = []
    for block in range(n_blocks):
        high, low, rest, core = block // 16, (block // 8) % 2, (block // 2) % 4, block % 2
        order.append((low * 2 + core, high * 4 + rest))
    return order


def split_units(one, two, n_blocks):
    rows, total = one.shape
    size = total // n_blocks

    def body(one_ref, two_ref, out_ref):
        for half, in_ref in enumerate((one_ref, two_ref)):
            for block, (quarter, at) in enumerate(unit_blocks(n_blocks)):
                out_ref[quarter, half * rows : (half + 1) * rows, at * size : (at + 1) * size] = in_ref[
                    :, block * size : (block + 1) * size
                ]

    return pl.pallas_call(
        body,
        out_shape=jax.ShapeDtypeStruct((4, 2 * rows, total // 4), one.dtype),
        cost_estimate=SHORT,
        name="split_units",
    )(one, two)


def matmul(left, right):
    return jnp.dot(left, right, preferred_element_type=F32)


def matmul_rows(left, right):
    return lax.dot_general(left, right, (((0,), (0,)), ((), ())), preferred_element_type=F32)


def matmul_cols(left, right):
    return lax.dot_general(left, right, (((1,), (1,)), ((), ())), preferred_element_type=F32)


def norm_forward(values, gain):
    inverse = lax.rsqrt(jnp.mean(values * values, axis=-1, keepdims=True) + EPSILON)
    return (values * inverse * gain, inverse)


def norm_backward(values, inverse, gain, grad_out):
    normed = values * inverse
    scaled = grad_out * gain
    grad_values = inverse * (scaled - normed * jnp.mean(scaled * normed, axis=-1, keepdims=True))
    return (grad_values, normed)


def rope_tables(seg_len):
    position = jnp.arange(seg_len).astype(F32)
    freqs = ROPE_BASE ** (-(2.0 * jnp.arange(HD // 2).astype(F32)) / HD)
    angle = position[:, None] * freqs[None, :]
    cosine, sine = jnp.cos(angle), jnp.sin(angle)
    return (jnp.concatenate([cosine, cosine], -1), jnp.concatenate([-sine, sine], -1))


def rope_heads(values, cosine, sine):
    half = HD // 2
    swapped = jnp.concatenate([values[..., half:], values[..., :half]], -1)
    return values * cosine[:, None, :] + swapped * sine[:, None, :]


def mask_kernel(n_cols, cols_ref, live_ref, out_ref, scratch):
    queries = cols_ref.shape[1]
    picks = cols_ref[0]
    pad = scratch.shape[0]
    high = lax.shift_right_arithmetic(picks, 7)
    low = jnp.bitwise_and(picks, LANES - 1)
    iota_high = lax.broadcasted_iota(jnp.int32, (pad, picks.shape[1]), 0)
    iota_low = lax.broadcasted_iota(jnp.int32, (LANES, picks.shape[1]), 0)
    for i in range(queries):
        hot_high = jnp.where(iota_high == high[i : i + 1, :], 1.0, 0.0).astype(BF)
        hot_low = jnp.where(iota_low == low[i : i + 1, :], 1.0, 0.0).astype(BF)
        scratch[:, i, :] = matmul_cols(hot_high, hot_low)
    out_ref[0, 0:n_cols] = jnp.where(scratch[0:n_cols] > 0.5, POS_BIG, NEG_BIG).astype(BF)
    row = lax.broadcasted_iota(jnp.int32, (queries, LANES), 0) + pl.program_id(1) * queries
    for part in range(out_ref.shape[1] - n_cols):
        col = lax.broadcasted_iota(jnp.int32, (queries, LANES), 1) + part * LANES
        live = live_ref[0, :, part * LANES : (part + 1) * LANES]
        allow = (col == row) | ((col < row) & (live == 1))
        out_ref[0, n_cols + part] = jnp.where(allow, POS_BIG, NEG_BIG).astype(BF)


def build_mask(columns, live, n_cols):
    rows, queries, picks = columns.shape
    block = 16
    pad = cdiv(n_cols, 8) * 8
    n_local = live.shape[2] // LANES
    return pl.pallas_call(
        lambda *refs: mask_kernel(n_cols, *refs),
        grid=(rows, queries // block),
        in_specs=[
            pl.BlockSpec((1, block, picks), lambda r, g: (r, g, 0)),
            pl.BlockSpec((1, 1, live.shape[2]), lambda r, g: (r, 0, 0)),
        ],
        out_specs=pl.BlockSpec((1, n_cols + n_local, block, LANES), lambda r, g: (r, 0, g, 0)),
        out_shape=jax.ShapeDtypeStruct((rows, n_cols + n_local, queries, LANES), BF),
        scratch_shapes=[pltpu.VMEM((pad, block, LANES), F32)],
        compiler_params=pltpu.CompilerParams(vmem_limit_bytes=VMEM_BYTES),
        cost_estimate=pl.CostEstimate(flops=12000000000, bytes_accessed=3000000, transcendentals=0),
        name="mask_build",
    )(columns, live)


def project_kernel(x_ref, wa_ref, wb_ref, cos_ref, sin_ref, q_ref, k_ref, v_ref, h_ref, inv_ref, gain_ref):
    quarter = q_ref.shape[2]

    @pl.when(pl.program_id(0) == 0)
    def gains():
        gain_ref[...] = jnp.transpose(wb_ref[:, quarter:].astype(F32), (1, 0))[0:8]

    x = x_ref[0].astype(F32)
    inverse = lax.rsqrt(jnp.mean(x * x, axis=-1, keepdims=True) + EPSILON)
    h = (x * inverse * gain_ref[0:1, :]).astype(BF)
    h_ref[0] = h
    inv_ref[0] = inverse
    turned = matmul(h, wa_ref[:, : 2 * quarter])
    for head in range(2 * quarter // HD):
        value = turned[:, head * HD : (head + 1) * HD]
        value = (value * cos_ref[...] + pltpu.roll(value, HD // 2, 1) * sin_ref[...]).astype(BF)
        if head < quarter // HD:
            q_ref[0, :, head * HD : (head + 1) * HD] = value
        else:
            at = head * HD - quarter
            k_ref[0, :, at : at + HD] = value
    v_ref[0] = matmul(h, wa_ref[:, 2 * quarter :]).astype(BF)


def project(x_all, w_a, w_b, cosine, sine):
    blocks, seg_len, width = x_all.shape
    quarter = w_a.shape[1] // 3
    whole = lambda array: pl.BlockSpec(array.shape, lambda r: (0, 0))
    head = pl.BlockSpec((1, seg_len, quarter), lambda r: (r, 0, 0))
    full = pl.BlockSpec((1, seg_len, width), lambda r: (r, 0, 0))
    out = jax.ShapeDtypeStruct((blocks, seg_len, quarter), BF)
    return pl.pallas_call(
        project_kernel,
        grid=(blocks,),
        in_specs=[full, whole(w_a), whole(w_b), whole(cosine), whole(sine)],
        out_specs=[head, head, head, full, pl.BlockSpec((1, seg_len, 1), lambda r: (r, 0, 0))],
        out_shape=[out, out, out, jax.ShapeDtypeStruct(x_all.shape, BF), jax.ShapeDtypeStruct((blocks, seg_len, 1), F32)],
        scratch_shapes=[pltpu.VMEM((8, width), F32)],
        compiler_params=pltpu.CompilerParams(vmem_limit_bytes=VMEM_BYTES),
        cost_estimate=SHORT,
        name="project",
    )(x_all, w_a, w_b, cosine, sine)


def plane_place():
    x, low, unused, y, core = place()
    return jnp.stack([x, y, 2 * low + core]).astype(jnp.int32)


def gradient(*entries):
    tokens, width = entries[0][0].shape
    n_blocks = lax.axis_size("seg")
    rows = width // n_blocks
    half = rows // 2
    sizes = [[entry[3] or right.shape[1] for right in entry[1]] for entry in entries]
    if rows % LANES:
        x, unused, unused, y, unused = place()
        outs = []
        for left, rights, way, columns in entries:
            if columns:
                rights = [cut(right, plane_place()[2] * columns, columns) for right in rights]
            full = jnp.concatenate([matmul_rows(left, right).astype(BF) for right in rights], 1)
            full = full.reshape(-1, 2, 2, half, full.shape[1])
            if way == "xy":
                near, side = halves(full, 1, x)
                near, side = halves(near, 1, y), halves(side, 1, y)
                parts = [near[0], side[0], near[1], side[1]]
            else:
                parts = halves(full, 1, x) if way == "x" else halves(full, 2, y)
            outs.append([part.reshape(-1, half, part.shape[-1]) for part in parts])
        return outs
    lefts = []
    for entry in entries:
        if not any(entry[0] is left for left in lefts):
            lefts.append(entry[0])
    which = [[entry[0] is left for left in lefts].index(True) for entry in entries]
    counts = [4 if entry[2] == "xy" else 2 for entry in entries]
    shapes = []
    for entry, size, count in zip(entries, sizes, counts):
        blocks = n_blocks // 2 if entry[2] == "xy" else n_blocks
        shapes += [(blocks, half, sum(size))] * count
    n_rights = sum(len(size) for size in sizes)

    def body(at_ref, *refs):
        left_refs, right_refs = refs[: len(lefts)], list(refs[len(lefts) : len(lefts) + n_rights])
        out_refs = list(refs[len(lefts) + n_rights :])
        pair = pl.program_id(0)
        turned = [jnp.transpose(ref[...]) for ref in left_refs]

        def by_row(value):
            upper, lower = value[:half], value[half:]
            return jnp.where(at_ref[1] == 0, upper, lower), jnp.where(at_ref[1] == 0, lower, upper)

        for entry, i, size, count in zip(entries, which, sizes, counts):
            outs, out_refs = out_refs[:count], out_refs[count:]
            start = 0
            for width_here in size:
                product = matmul(turned[i], right_refs.pop(0)[...]).astype(BF)
                span = slice(start, start + width_here)
                start += width_here
                first, second = product[:rows], product[rows:]
                if entry[2] == "y":
                    for side, value in enumerate((first, second)):
                        outs[0][2 * pair + side, :, span], outs[1][2 * pair + side, :, span] = by_row(value)
                    continue
                same = jnp.where(at_ref[0] == 0, first, second)
                other = jnp.where(at_ref[0] == 0, second, first)
                if entry[2] == "x":
                    for ref, value in zip(outs, (same, other)):
                        ref[2 * pair, :, span] = value[:half]
                        ref[2 * pair + 1, :, span] = value[half:]
                else:
                    outs[0][pair, :, span], outs[2][pair, :, span] = by_row(same)
                    outs[1][pair, :, span], outs[3][pair, :, span] = by_row(other)

    in_specs = [pl.BlockSpec((tokens, 2 * rows), lambda i, at: (0, i))] * len(lefts)
    for entry, size in zip(entries, sizes):
        column = (lambda i, at: (0, at[2])) if entry[3] else (lambda i, at: (0, 0))
        in_specs += [pl.BlockSpec((tokens, width_here), column) for width_here in size]
    outs = pl.pallas_call(
        body,
        grid_spec=pltpu.PrefetchScalarGridSpec(
            num_scalar_prefetch=1,
            grid=(n_blocks // 2,),
            in_specs=in_specs,
            out_specs=[pl.BlockSpec(shape, lambda i, at: (0, 0, 0)) for shape in shapes],
        ),
        out_shape=[jax.ShapeDtypeStruct(shape, BF) for shape in shapes],
        compiler_params=pltpu.CompilerParams(vmem_limit_bytes=VMEM_BYTES),
        cost_estimate=SHORT,
        name="gradient",
    )(plane_place(), *lefts, *[right for entry in entries for right in entry[1]])
    groups = []
    for count in counts:
        groups.append(outs[:count])
        outs = outs[count:]
    return groups


def split_sums(keep, recv, way):
    n_blocks, rows, cols = keep.shape

    def body(at_ref, keep_ref, recv_ref, mine_ref, give_ref):
        side = at_ref[1] if way == "y" else at_ref[0]
        for block in range(n_blocks // 2):
            for at, out_ref in ((2 * block + side, mine_ref), (2 * block + 1 - side, give_ref)):
                out_ref[block] = (keep_ref[at].astype(F32) + recv_ref[at].astype(F32)).astype(BF)

    vmem = pl.BlockSpec(memory_space=pltpu.VMEM)
    return pl.pallas_call(
        body,
        in_specs=[pl.BlockSpec(memory_space=pltpu.SMEM)] + [vmem] * 2,
        out_specs=[vmem] * 2,
        out_shape=[jax.ShapeDtypeStruct((n_blocks // 2, rows, cols), BF)] * 2,
        compiler_params=pltpu.CompilerParams(vmem_limit_bytes=VMEM_BYTES),
        cost_estimate=SHORT,
        name="split_sums",
    )(plane_place(), keep, recv)


def gradient_units(left, right):
    tokens, width = left.shape
    n_high = lax.axis_size("seg") // 4
    rows = width // (4 * n_high)
    cols = right.shape[1]
    step = 256
    if rows % 8:
        full = matmul_rows(left, right).astype(BF).reshape(-1, 2, 2, rows, cols)
        return halves(full, 1, place()[0])

    def body(at_ref, left_ref, right_ref, keep_ref, give_ref):
        product = matmul_rows(left_ref[...], right_ref[...])
        for high in range(n_high):
            for y in range(2):
                zero, one = [
                    product[(high * 4 + x * 2 + y) * rows : (high * 4 + x * 2 + y + 1) * rows] for x in range(2)
                ]
                keep_ref[high, y] = jnp.where(at_ref[0] == 0, zero, one).astype(BF)
                give_ref[high, y] = jnp.where(at_ref[0] == 0, one, zero).astype(BF)

    shape = (n_high, 2, rows, cols)
    return pl.pallas_call(
        body,
        grid_spec=pltpu.PrefetchScalarGridSpec(
            num_scalar_prefetch=1,
            grid=(cols // step,),
            in_specs=[
                pl.BlockSpec((tokens, width), lambda i, at: (0, 0)),
                pl.BlockSpec((tokens, step), lambda i, at: (0, i)),
            ],
            out_specs=[pl.BlockSpec((n_high, 2, rows, step), lambda i, at: (0, 0, 0, i))] * 2,
        ),
        out_shape=[jax.ShapeDtypeStruct(shape, BF)] * 2,
        compiler_params=pltpu.CompilerParams(vmem_limit_bytes=VMEM_BYTES),
        cost_estimate=SHORT,
        name="gradient_units",
    )(plane_place(), left, right)


def group_place():
    unused, low, high, unused, core = place()
    return jnp.stack([2 * high + low, low, core]).astype(jnp.int32)


def plane_sort(*groups, units=()):
    sizes = [group[0].shape[-1] for group in groups]
    rows, cols = groups[0][0].shape[1], sum(sizes)
    shapes = [(rows, cols)] * 4
    if units:
        unit_rows = units[0].shape[1]
        below = cdiv(unit_rows, 16) * 16
        shapes = [(rows + below if way == 2 else rows, cols) for way in range(4)] + [(unit_rows, cols)]

    def body(at_ref, *refs):
        in_refs, out_refs = list(refs[: -len(shapes)]), refs[-len(shapes) :]
        unit_refs = in_refs[len(in_refs) - len(units) :]
        for way in range(4):
            start = 0
            left = list(in_refs)
            for size, group in zip(sizes, groups):
                total = None
                for unused in group:
                    part = left.pop(0)[at_ref[0] ^ way].astype(F32)
                    total = part if total is None else total + part
                out_refs[way][0:rows, start : start + size] = total.astype(BF)
                start += size
        if units:
            high = lax.shift_right_logical(at_ref[0], 1)
            own = sum(ref[high].astype(F32) for ref in unit_refs)
            give = sum(ref[1 - high].astype(F32) for ref in unit_refs)
            out_refs[4][...] = own.astype(BF)
            give = jnp.concatenate([give, jnp.zeros((below - unit_rows, cols), F32)], 0)
            out_refs[2][rows : rows + below, :] = give.astype(BF)

    vmem = pl.BlockSpec(memory_space=pltpu.VMEM)
    arrays = [array for group in groups for array in group] + list(units)
    return pl.pallas_call(
        body,
        in_specs=[pl.BlockSpec(memory_space=pltpu.SMEM)] + [vmem] * len(arrays),
        out_specs=[vmem] * len(shapes),
        out_shape=[jax.ShapeDtypeStruct(shape, BF) for shape in shapes],
        compiler_params=pltpu.CompilerParams(vmem_limit_bytes=VMEM_BYTES),
        cost_estimate=SHORT,
        name="plane_sort",
    )(group_place(), *arrays)


def z_merge(kept, from_1, from_2, from_3):
    rows, cols = kept.shape
    half = rows // 2

    def body(at_ref, kept_ref, one_ref, two_ref, three_ref, keep_ref, give_ref):
        same = kept_ref[...].astype(F32) + two_ref[0:rows, :].astype(F32)
        other = one_ref[...].astype(F32) + three_ref[...].astype(F32)
        for quarter, value in ((at_ref[1], same), (1 - at_ref[1], other)):
            upper, lower = value[:half], value[half:]
            keep_ref[quarter] = jnp.where(at_ref[2] == 0, upper, lower).astype(BF)
            give_ref[quarter] = jnp.where(at_ref[2] == 0, lower, upper).astype(BF)

    vmem = pl.BlockSpec(memory_space=pltpu.VMEM)
    return pl.pallas_call(
        body,
        in_specs=[pl.BlockSpec(memory_space=pltpu.SMEM)] + [vmem] * 4,
        out_specs=[vmem] * 2,
        out_shape=[jax.ShapeDtypeStruct((2, half, cols), BF)] * 2,
        compiler_params=pltpu.CompilerParams(vmem_limit_bytes=VMEM_BYTES),
        cost_estimate=SHORT,
        name="z_merge",
    )(group_place(), kept, from_1, from_2, from_3)


def join_quarters(mine, recv, core_ref, start, size, z_low, core):
    return jnp.where(
        core_ref[2] == core, mine[z_low, :, start : start + size], recv[z_low, :, start : start + size]
    ).astype(F32)


def join_columns(mine, recv, weights, gain, n_matrices):
    rows, cols = mine.shape[1:]
    size = cols // n_matrices

    def body(at_ref, mine_ref, recv_ref, gain_ref, *refs):
        weight_refs, out_refs = refs[: len(weights)], refs[len(weights) :]
        total = jnp.zeros((rows, 1), F32)
        for i in range(n_matrices):
            for z_low in range(2):
                for core in range(2):
                    at = (2 * z_low + core) * size
                    value = join_quarters(mine_ref, recv_ref, at_ref, i * size, size, z_low, core)
                    out_refs[i][:, at : at + size] = value
                    if i < len(weights):
                        product = value * weight_refs[i][:, at : at + size].astype(F32)
                        total = total + jnp.sum(product, axis=1, keepdims=True)
        out_refs[-1][...] = total / gain_ref[...]

    vmem = pl.BlockSpec(memory_space=pltpu.VMEM)
    outs = pl.pallas_call(
        body,
        in_specs=[pl.BlockSpec(memory_space=pltpu.SMEM)] + [vmem] * (3 + len(weights)),
        out_specs=[vmem] * (n_matrices + 1),
        out_shape=[jax.ShapeDtypeStruct((rows, 4 * size), F32)] * n_matrices + [jax.ShapeDtypeStruct((rows, 1), F32)],
        cost_estimate=SHORT,
        name="join_columns",
    )(group_place(), mine, recv, gain.astype(F32)[:, None], *weights)
    return outs[:-1] + [outs[-1][:, 0]] if isinstance(outs, list) else list(outs[:-1]) + [outs[-1][:, 0]]


def join_units(mine, recv, weights, gain, n_blocks):
    rows, both = mine.shape[1:]
    quarter_size = both // 2
    size = 4 * quarter_size // n_blocks

    def body(at_ref, mine_ref, recv_ref, gain_ref, one_weight, two_weight, one_ref, two_ref, total_ref):
        total = jnp.zeros((rows, 1), F32)
        for half, (out_ref, weight_ref) in enumerate(((one_ref, one_weight), (two_ref, two_weight))):
            for block, (quarter, at) in enumerate(unit_blocks(n_blocks)):
                start = half * quarter_size + at * size
                out_ref[:, block * size : (block + 1) * size] = join_quarters(
                    mine_ref, recv_ref, at_ref, start, size, quarter // 2, quarter % 2
                )
            total = total + jnp.sum(out_ref[...] * weight_ref[...].astype(F32), axis=1, keepdims=True)
        total_ref[...] = total / gain_ref[...]

    vmem = pl.BlockSpec(memory_space=pltpu.VMEM)
    one, two, total = pl.pallas_call(
        body,
        in_specs=[pl.BlockSpec(memory_space=pltpu.SMEM)] + [vmem] * 5,
        out_specs=[vmem] * 3,
        out_shape=[jax.ShapeDtypeStruct((rows, 4 * quarter_size), F32)] * 2 + [jax.ShapeDtypeStruct((rows, 1), F32)],
        cost_estimate=SHORT,
        name="join_units",
    )(group_place(), mine, recv, gain.astype(F32)[:, None], *weights)
    return one, two, total[:, 0]


def pair_add(one, two):
    def body(at_ref, one_ref, two_ref, own_ref, give_ref):
        for way, out_ref in enumerate((own_ref, give_ref)):
            at = at_ref[1] ^ way
            out_ref[...] = (one_ref[at].astype(F32) + two_ref[at].astype(F32)).astype(BF)

    vmem = pl.BlockSpec(memory_space=pltpu.VMEM)
    return pl.pallas_call(
        body,
        in_specs=[pl.BlockSpec(memory_space=pltpu.SMEM)] + [vmem] * 2,
        out_specs=[vmem] * 2,
        out_shape=[jax.ShapeDtypeStruct(one.shape[1:], BF)] * 2,
        compiler_params=pltpu.CompilerParams(vmem_limit_bytes=VMEM_BYTES),
        cost_estimate=SHORT,
        name="pair_add",
    )(group_place(), one, two)


def back_project(lefts, weights, transposed=True):
    block = lefts[0].shape[0] // 4
    out = weights[0].shape[0] if transposed else weights[0].shape[1]

    def body(*refs):
        left_refs, weight_refs = refs[: len(lefts)], refs[len(lefts) : 2 * len(lefts)]
        keep_ref, give_ref = refs[2 * len(lefts) :]
        total = None
        for left_ref, weight_ref in zip(left_refs, weight_refs):
            part = (matmul_cols if transposed else matmul)(left_ref[...], weight_ref[...])
            total = part if total is None else total + part
        total = total.astype(BF)
        for i in range(4):
            (keep_ref, give_ref)[i % 2][i // 2] = total[i * block : (i + 1) * block]

    return pl.pallas_call(
        body,
        in_specs=[pl.BlockSpec(memory_space=pltpu.VMEM)] * (2 * len(lefts)),
        out_specs=[pl.BlockSpec(memory_space=pltpu.VMEM)] * 2,
        out_shape=[jax.ShapeDtypeStruct((2, block, out), BF)] * 2,
        compiler_params=pltpu.CompilerParams(vmem_limit_bytes=VMEM_BYTES),
        cost_estimate=SHORT,
        name="back_project",
    )(*lefts, *weights)


def join_four(mine, recv, of_tokens):
    rows, size = mine.shape[1:]
    block = rows // 4

    def body(at_ref, mine_ref, recv_ref, out_ref):
        for z_low in range(2):
            side = at_ref[1] ^ z_low
            for core in range(2):
                at = (2 * z_low + core) * size
                for i in range(4):
                    j = i ^ 1 if of_tokens else i
                    ours = mine_ref[side, i * block : (i + 1) * block]
                    theirs = recv_ref[side, j * block : (j + 1) * block]
                    out_ref[i * block : (i + 1) * block, at : at + size] = jnp.where(at_ref[2] == core, ours, theirs)

    vmem = pl.BlockSpec(memory_space=pltpu.VMEM)
    return pl.pallas_call(
        body,
        in_specs=[pl.BlockSpec(memory_space=pltpu.SMEM)] + [vmem] * 2,
        out_specs=vmem,
        out_shape=jax.ShapeDtypeStruct((rows, 4 * size), mine.dtype),
        compiler_params=pltpu.CompilerParams(vmem_limit_bytes=VMEM_BYTES),
        cost_estimate=SHORT,
        name="join_four",
    )(group_place(), mine, recv)


def branch_back(mine, recv, x_one, gain, g_mine, g_recv, w_out):
    blocks, seg_len, width = x_one.shape
    quarter = width // 4

    def body(at_ref, mine_ref, recv_ref, x_ref, gain_ref, g_ref, g_recv_ref, w_ref, branch_ref, att_ref, own_ref):
        block = pl.program_id(0)
        grad = jnp.where(block % 2 == 0, mine_ref[0], recv_ref[0]).astype(F32)
        passed = jnp.where(block % 2 == 0, g_ref[0], g_recv_ref[0]).astype(F32)
        values = x_ref[0]
        inverse = lax.rsqrt(jnp.mean(values * values, axis=-1, keepdims=True) + EPSILON)
        normed = values * inverse
        scaled = grad * gain_ref[...]
        mean = jnp.mean(scaled * normed, axis=-1, keepdims=True)
        total = passed + inverse * (scaled - normed * mean)
        low = total.astype(BF)
        branch_ref[0] = low
        att_ref[0] = matmul_cols(low, w_ref[...]).astype(BF)

        @pl.when(block == 2 * at_ref[1])
        def own():
            own_ref[...] = total

    pair = pl.BlockSpec((1, seg_len, width), lambda i, at: (i // 2, 0, 0))
    full = pl.BlockSpec((1, seg_len, width), lambda i, at: (i, 0, 0))
    return pl.pallas_call(
        body,
        grid_spec=pltpu.PrefetchScalarGridSpec(
            num_scalar_prefetch=1,
            grid=(blocks,),
            in_specs=[
                pair,
                pair,
                full,
                pl.BlockSpec((1, width), lambda i, at: (0, 0)),
                pair,
                pair,
                pl.BlockSpec((quarter, width), lambda i, at: (2 * at[1] + at[2], 0)),
            ],
            out_specs=[
                full,
                pl.BlockSpec((1, seg_len, quarter), lambda i, at: (i, 0, 0)),
                pl.BlockSpec((seg_len, width), lambda i, at: (0, 0)),
            ],
        ),
        out_shape=[
            jax.ShapeDtypeStruct((blocks, seg_len, width), BF),
            jax.ShapeDtypeStruct((blocks, seg_len, quarter), BF),
            jax.ShapeDtypeStruct((seg_len, width), F32),
        ],
        compiler_params=pltpu.CompilerParams(vmem_limit_bytes=VMEM_BYTES),
        cost_estimate=SHORT,
        name="branch_back",
    )(group_place(), mine, recv, x_one, gain, g_mine, g_recv, w_out)


def add_kernel(one, two):
    def body(one_ref, two_ref, out_ref):
        out_ref[...] = (one_ref[...].astype(F32) + two_ref[...].astype(F32)).astype(BF)

    return pl.pallas_call(
        body,
        in_specs=[pl.BlockSpec(memory_space=pltpu.VMEM)] * 2,
        out_specs=pl.BlockSpec(memory_space=pltpu.VMEM),
        out_shape=jax.ShapeDtypeStruct(one.shape, BF),
        compiler_params=pltpu.CompilerParams(vmem_limit_bytes=VMEM_BYTES),
        cost_estimate=SHORT,
        name="add_kernel",
    )(one, two)


def add_low(one, two):
    return (one.astype(F32) + two.astype(F32)).astype(BF)


def lane_blocks(value):
    return [value[:, i : i + LANES] for i in range(0, value.shape[1], LANES)]


PIECES = ((0, 0), (0, 1), (1, 0), (1, 1), (2, 0), (3, 0), (2, 1))
N_COMMON = 5
N_GROUPS = 4


def forward_kernel(q_ref, k_ref, v_ref, mine_ref, other_ref, *refs):
    key_refs, value_refs = refs[:N_GROUPS], refs[N_GROUPS : 2 * N_GROUPS]
    o_ref, of_ref, p_ref, pl_ref, inv_ref, s_ref, top_ref, total_ref, acc_ref = refs[2 * N_GROUPS :]
    scale = HD ** (-0.5)
    upper = pl.program_id(1) >= 2
    queries = q_ref[0]
    seg_len = queries.shape[0]
    per = key_refs[0].shape[1] // LANES
    first = pl.program_id(1) % 2 == 0

    def bias(at):
        return jnp.where(first, mine_ref[0, at], other_ref[0, at]).astype(F32)

    local_bias = jnp.concatenate([bias(len(PIECES) * per + i) for i in range(cdiv(seg_len, LANES))], 1)
    s_local = jnp.minimum(matmul_cols(queries, k_ref[0]) * scale, local_bias[:, :seg_len])

    def score(t, top):
        group, low = PIECES[t]
        parts = lane_blocks(matmul_cols(queries, key_refs[group][low]) * scale)
        for i in range(per):
            part = jnp.minimum(parts[i], bias(t * per + i))
            s_ref[t, :, i * LANES : (i + 1) * LANES] = part
            top = part if top is None else jnp.maximum(top, part)
        return top

    top = None
    for t in range(N_COMMON):
        top = score(t, top)
    top_ref[...] = top

    @pl.when(upper)
    def more_scores():
        more = top_ref[...]
        for t in range(N_COMMON, len(PIECES)):
            more = score(t, more)
        top_ref[...] = more

    row_max = jnp.maximum(
        jnp.max(s_local, axis=-1, keepdims=True), jnp.max(top_ref[...], axis=-1, keepdims=True)
    )
    e_local = jnp.exp(s_local - row_max)
    low_local = e_local.astype(BF)
    pl_ref[0, 0] = low_local

    def weigh(t, total, acc):
        group, low = PIECES[t]
        expo = jnp.exp(s_ref[t] - row_max)
        for part in lane_blocks(expo):
            total = part if total is None else total + part
        chances = expo.astype(BF)
        p_ref[0, 0, t] = chances
        return total, acc + matmul(chances, value_refs[group][low])

    total, acc = None, matmul(low_local, v_ref[0])
    for t in range(N_COMMON):
        total, acc = weigh(t, total, acc)
    total_ref[...] = total
    acc_ref[...] = acc

    @pl.when(upper)
    def more_values():
        total, acc = total_ref[...], acc_ref[...]
        for t in range(N_COMMON, len(PIECES)):
            total, acc = weigh(t, total, acc)
        total_ref[...] = total
        acc_ref[...] = acc

    row_total = jnp.sum(e_local, axis=-1, keepdims=True) + jnp.sum(total_ref[...], axis=-1, keepdims=True)
    inverse = 1.0 / row_total
    out = acc_ref[...] * inverse
    of_ref[0] = out
    o_ref[0] = out.astype(BF)
    inv_ref[0, 0] = inverse


def backward_local_kernel(do_ref, of_ref, q_ref, k_ref, v_ref, inv_ref, pl_ref, cos_ref, sin_ref, dkv_ref, dq_ref):
    scale = HD ** (-0.5)
    d_out = do_ref[0]
    delta = jnp.sum(d_out.astype(F32) * of_ref[0], axis=-1, keepdims=True)
    chances = pl_ref[0, 0].astype(F32) * inv_ref[0, 0]
    ds = (chances * (matmul_cols(d_out, v_ref[0]) - delta)).astype(BF)
    dq_ref[0] = matmul(ds, k_ref[0])
    dk = matmul_rows(ds, q_ref[0])
    dkv_ref[0, 0] = ((dk * cos_ref[...] - pltpu.roll(dk, HD // 2, 1) * sin_ref[...]) * scale).astype(BF)
    dkv_ref[1, 0] = matmul_rows(chances.astype(BF), d_out).astype(BF)


def backward_kernel(do_ref, of_ref, local_ref, inv_ref, p_ref, cos_ref, sin_ref, *refs):
    key_refs, value_refs = refs[:N_GROUPS], refs[N_GROUPS : 2 * N_GROUPS]
    out_ref, dq_ref = refs[2 * N_GROUPS :]
    scale = HD ** (-0.5)
    upper = pl.program_id(1) >= 2
    d_out = do_ref[0]
    inverse = inv_ref[0, 0]
    delta = jnp.sum(d_out.astype(F32) * of_ref[0], axis=-1, keepdims=True)

    def piece(t, dq):
        group, low = PIECES[t]
        dp = matmul_cols(d_out, value_refs[group][low])
        ds = (p_ref[0, 0, t].astype(F32) * ((dp - delta) * inverse)).astype(BF)
        return dq + matmul(ds, key_refs[group][low])

    dq = local_ref[0]
    for t in range(N_COMMON):
        dq = piece(t, dq)
    dq_ref[...] = dq

    @pl.when(upper)
    def more():
        dq = dq_ref[...]
        for t in range(N_COMMON, len(PIECES)):
            dq = piece(t, dq)
        dq_ref[...] = dq

    dq = dq_ref[...]
    out_ref[0] = ((dq * cos_ref[...] - pltpu.roll(dq, HD // 2, 1) * sin_ref[...]) * scale).astype(BF)


def attention_specs(piece_rows, seg_len):
    head = pl.BlockSpec((1, seg_len, HD), lambda h, r: (r, 0, h))
    piece = pl.BlockSpec((2, piece_rows, HD), lambda h, r: (0, 0, h))
    p_spec = pl.BlockSpec((1, 1, len(PIECES), seg_len, piece_rows), lambda h, r: (r, h, 0, 0, 0))
    pl_spec = pl.BlockSpec((1, 1, seg_len, seg_len), lambda h, r: (r, h, 0, 0))
    inv_spec = pl.BlockSpec((1, 1, seg_len, 1), lambda h, r: (r, h, 0, 0))
    return head, piece, p_spec, pl_spec, inv_spec


def attention_forward(queries, keys, values, mask, other_mask, key_pieces, value_pieces):
    blocks, seg_len, width = queries.shape
    heads = width // HD
    piece_rows = key_pieces[0].shape[1]
    head, piece, p_spec, pl_spec, inv_spec = attention_specs(piece_rows, seg_len)
    return pl.pallas_call(
        forward_kernel,
        grid=(heads, blocks),
        in_specs=[
            head,
            head,
            head,
            pl.BlockSpec((1,) + mask.shape[1:], lambda h, r: (r // 2, 0, 0, 0)),
            pl.BlockSpec((1,) + mask.shape[1:], lambda h, r: (r // 2, 0, 0, 0)),
        ]
        + [piece] * (2 * N_GROUPS),
        out_specs=[head, head, p_spec, pl_spec, inv_spec],
        out_shape=[
            jax.ShapeDtypeStruct(queries.shape, BF),
            jax.ShapeDtypeStruct(queries.shape, F32),
            jax.ShapeDtypeStruct((blocks, heads, len(PIECES), seg_len, piece_rows), BF),
            jax.ShapeDtypeStruct((blocks, heads, seg_len, seg_len), BF),
            jax.ShapeDtypeStruct((blocks, heads, seg_len, 1), F32),
        ],
        scratch_shapes=[
            pltpu.VMEM((len(PIECES), seg_len, piece_rows), F32),
            pltpu.VMEM((seg_len, LANES), F32),
            pltpu.VMEM((seg_len, LANES), F32),
            pltpu.VMEM((seg_len, HD), F32),
        ],
        compiler_params=pltpu.CompilerParams(vmem_limit_bytes=VMEM_BYTES),
        cost_estimate=SHORT,
        name="attention_forward",
    )(queries, keys, values, mask, other_mask, *key_pieces, *value_pieces)


def attention_backward_local(d_out, out_f32, queries, keys, values, inverse, p_local, cosine, sine):
    blocks, seg_len, width = queries.shape
    head, unused, unused, pl_spec, inv_spec = attention_specs(seg_len, seg_len)
    table = pl.BlockSpec((seg_len, HD), lambda h, r: (0, 0))
    return pl.pallas_call(
        backward_local_kernel,
        grid=(width // HD, blocks),
        in_specs=[head, head, head, head, head, inv_spec, pl_spec, table, table],
        out_specs=[pl.BlockSpec((2, 1, seg_len, HD), lambda h, r: (0, r, 0, h)), head],
        out_shape=[
            jax.ShapeDtypeStruct((2, blocks, seg_len, width), BF),
            jax.ShapeDtypeStruct(queries.shape, F32),
        ],
        compiler_params=pltpu.CompilerParams(vmem_limit_bytes=VMEM_BYTES),
        cost_estimate=SHORT,
        name="attention_backward_local",
    )(d_out, out_f32, queries, keys, values, inverse, p_local, cosine, sine)


def attention_backward(d_out, out_f32, dq_local, inverse, p_memory, cosine, sine, key_pieces, value_pieces):
    blocks, seg_len, width = d_out.shape
    heads = width // HD
    piece_rows = key_pieces[0].shape[1]
    head, piece, p_spec, unused, inv_spec = attention_specs(piece_rows, seg_len)
    table = pl.BlockSpec((seg_len, HD), lambda h, r: (0, 0))
    return pl.pallas_call(
        backward_kernel,
        grid=(heads, blocks),
        in_specs=[head, head, head, inv_spec, p_spec, table, table] + [piece] * (2 * N_GROUPS),
        out_specs=head,
        out_shape=jax.ShapeDtypeStruct((blocks, seg_len, width), BF),
        scratch_shapes=[pltpu.VMEM((seg_len, HD), F32)],
        compiler_params=pltpu.CompilerParams(vmem_limit_bytes=VMEM_BYTES),
        cost_estimate=SHORT,
        name="attention_backward",
    )(d_out, out_f32, dq_local, inverse, p_memory, cosine, sine, *key_pieces, *value_pieces)


def allow_local_of(live):
    seg_len = live.shape[-1]
    position = jnp.arange(seg_len, dtype=jnp.int32)
    same = position[None, :] == position[:, None]
    return same[None] | ((position[None, :] < position[:, None])[None] & (live == 1))


def split_heads(value):
    rows, seg_len, width = value.shape
    return value.reshape(rows, seg_len, width // HD, HD)


def stream_forward(queries, keys, values, live, allow, memory):
    scale = HD ** (-0.5)
    q4, k4, v4 = split_heads(queries), split_heads(keys), split_heads(values)
    scores = jnp.einsum("rqhd,rkhd->rhqk", q4, k4, preferred_element_type=F32) * scale
    scores = jnp.where(allow_local_of(live)[:, None], scores, NEG_BIG)
    row_max = jnp.max(scores, axis=-1)
    expo = jnp.exp(scores - row_max[..., None])
    state = (
        row_max,
        jnp.sum(expo, axis=-1),
        jnp.einsum("rhqk,rkhd->rhqd", expo.astype(BF), v4, preferred_element_type=F32),
    )

    def step(running, item):
        row_max, row_total, acc = running
        block, allowed = item
        k3 = block[0].reshape(block.shape[1], -1, HD)
        v3 = block[1].reshape(block.shape[1], -1, HD)
        scores = jnp.einsum("rqhd,khd->rhqk", q4, k3, preferred_element_type=F32) * scale
        scores = jnp.where(allowed[:, None] > 0, scores, NEG_BIG)
        new_max = jnp.maximum(row_max, jnp.max(scores, axis=-1))
        shrink = jnp.exp(row_max - new_max)
        expo = jnp.exp(scores - new_max[..., None])
        acc = acc * shrink[..., None] + jnp.einsum(
            "rhqk,khd->rhqd", expo.astype(BF), v3, preferred_element_type=F32
        )
        return (new_max, row_total * shrink + jnp.sum(expo, axis=-1), acc), None

    (row_max, row_total, acc), unused = lax.scan(step, state, (memory, allow))
    out = (acc / row_total[..., None]).transpose(0, 2, 1, 3).reshape(queries.shape)
    return out.astype(BF), out, row_max + jnp.log(row_total)


def stream_backward(d_out, out_f32, queries, keys, values, live, log_total, allow, memory, cosine, sine):
    scale = HD ** (-0.5)
    q4, k4, v4, d4 = split_heads(queries), split_heads(keys), split_heads(values), split_heads(d_out)
    delta = jnp.sum(d4.astype(F32) * split_heads(out_f32), axis=-1).transpose(0, 2, 1)
    scores = jnp.einsum("rqhd,rkhd->rhqk", q4, k4, preferred_element_type=F32) * scale
    scores = jnp.where(allow_local_of(live)[:, None], scores, NEG_BIG)
    chances = jnp.exp(scores - log_total[..., None])
    dp = jnp.einsum("rqhd,rkhd->rhqk", d4, v4, preferred_element_type=F32)
    ds = (chances * (dp - delta[..., None])).astype(BF)
    dq = jnp.einsum("rhqk,rkhd->rqhd", ds, k4, preferred_element_type=F32)
    dk = jnp.einsum("rhqk,rqhd->rkhd", ds, q4, preferred_element_type=F32)
    dv = jnp.einsum("rhqk,rqhd->rkhd", chances.astype(BF), d4, preferred_element_type=F32)

    def step(running, item):
        block, allowed = item
        k3 = block[0].reshape(block.shape[1], -1, HD)
        v3 = block[1].reshape(block.shape[1], -1, HD)
        scores = jnp.einsum("rqhd,khd->rhqk", q4, k3, preferred_element_type=F32) * scale
        scores = jnp.where(allowed[:, None] > 0, scores, NEG_BIG)
        chances = jnp.exp(scores - log_total[..., None])
        dp = jnp.einsum("rqhd,khd->rhqk", d4, v3, preferred_element_type=F32)
        ds = (chances * (dp - delta[..., None])).astype(BF)
        return running + jnp.einsum("rhqk,khd->rqhd", ds, k3, preferred_element_type=F32), None

    dq, unused = lax.scan(step, dq, (memory, allow))

    def back(value):
        turned = rope_heads(value.reshape((-1,) + value.shape[2:]), jnp.tile(cosine, (value.shape[0], 1)), -jnp.tile(sine, (value.shape[0], 1)))
        return (turned * scale).reshape(queries.shape).astype(BF)

    return jnp.stack([back(dq), back(dk), dv.reshape(queries.shape).astype(BF)])


def local(
    layer_input,
    live,
    knn_index,
    mem_keys,
    mem_values,
    gain_attn,
    w_query,
    w_key,
    w_value,
    w_out,
    gain_ffn,
    w_gate,
    w_up,
    w_down,
    cotangent,
):
    seg_len, width = layer_input.shape[1:]
    quarter = width // 4
    n_seg = lax.axis_size("seg")
    n_devices = n_seg * lax.axis_size("rep")
    tokens = seg_len * n_seg
    n_high = n_seg // 4
    x, low, high, y, core = place()
    use_kernel = n_high <= KERNEL_HIGH
    kv_rows = 2 * seg_len
    group_tokens = 4 * seg_len

    def by_quarter(value):
        return [value[:, i * quarter : (i + 1) * quarter] for i in range(4)]

    gains = jnp.concatenate(
        [gain_attn[:, None], gain_ffn[:, None], jnp.zeros((gain_attn.shape[0], LANES - 2), BF)], 1
    )
    stacked = [by_quarter(w) for w in (w_query, w_key, w_value, w_out)]
    qo = jnp.stack([jnp.concatenate([s[i] for s in stacked] + [gains], 1) for i in range(4)])

    def core_quarters(value, side):
        return jnp.stack([cut(value, side * quarter, quarter), cut(value, (2 + side) * quarter, quarter)])

    def core_memory(side):
        return jnp.stack([core_quarters(mem_keys[0], side), core_quarters(mem_values[0], side)])

    coded = knn_index[0] * 2 + live[0][:, None]
    qo = qo.reshape(2, 2, -1, qo.shape[-1])
    qo_keep, qo_give = halves(qo, 1, core)
    kv_keep, kv_give = core_memory(core), core_memory(1 - core)
    qo_recv, kv_recv, coded_recv = flip_core(qo_give), flip_core(kv_give), flip_z(coded)
    qo_keep, kv_keep, coded, qo_recv, kv_recv, coded_recv, w_gate_, w_up_ = fence(
        qo_keep, kv_keep, coded, qo_recv, kv_recv, coded_recv, w_gate, w_up
    )

    qo_keep, qo_give = halves(ordered(qo_keep, qo_recv, core, 1), 0, low)
    kv_keep, kv_give = halves(ordered(kv_keep, kv_recv, core, 2), 1, low)
    coded = ordered(coded[None], coded_recv[None], low, 0)
    kv_recv = flip_z(kv_give)
    qo_near = flip_z(qo_give)
    down_w = w_down[None, None, None, None]
    x_own = layer_input[0]
    gate_up = split_units(w_gate_, w_up_, n_devices).reshape(2, 2, 2, -1, w_gate.shape[1] // 4)

    def places_of(codes, row_core):
        picks = lax.shift_right_arithmetic(codes, 1)
        pair = picks >= tokens
        slot = jnp.where(pair, picks - tokens, picks)
        slot_seg = slot // seg_len
        kv_row = jnp.bitwise_xor(pair.astype(jnp.int32), row_core)
        return picks, slot_seg, kv_row * seg_len + (slot - slot_seg * seg_len)

    split = 3 * quarter
    g_own = cotangent[0]
    cosine, sine = rope_tables(seg_len)
    if use_kernel:
        qo_far, qo_side = flip(qo_keep, "seg", 4), flip(qo_give, "seg", 6)
        picks, slot_seg, within = places_of(coded, core)
        slot_x, slot_low = slot_seg % 2, (slot_seg // 2) % 2
        same_x = slot_x == x
        in_group = jnp.where(same_x, 5, 4 + 2 * slot_low)
        before = jnp.where(same_x, 0, 2) + slot_low
        piece_no = jnp.where(slot_seg // 4 == high, in_group, before)
        columns = jnp.where(picks >= 0, piece_no * kv_rows + within, -1)
        live_two = jnp.bitwise_and(coded[:, :, 0], 1)[:, None, :]
        live_two = jnp.pad(live_two, ((0, 0), (0, 0), (0, cdiv(seg_len, LANES) * LANES - seg_len)))
        down_recv = flip(down_w, "seg", 4)
        (
            qo_keep, qo_near, qo_far, qo_side, kv_keep, kv_recv, x_own, gate_up, columns, live_two, down_w, down_recv
        ) = fence(
            qo_keep, qo_near, qo_far, qo_side, kv_keep, kv_recv, x_own, gate_up, columns, live_two, down_w, down_recv
        )

        pieces = ordered(kv_keep[:, None], kv_recv[:, None], low, 1)
        own_k, own_v = pieces[0], pieces[1]
        near = ordered(qo_keep[None, None], qo_near[None, None], low, 1)
        far = ordered(qo_far[None, None], qo_side[None, None], low, 1)
        qo = ordered(near, far, high, 0)[:, :, None, None]
        qo_a, qo_b = qo[..., :split], qo[..., split:]
        up_high = [(i, i + 4) for i in range(n_seg - 4)]

        def cross(value):
            return lax.ppermute(value, "seg", up_high)

        cross_k, side_k = cross(own_k), flip_x(own_k)
        a_recv, b_recv = flip_x(qo_a), flip_y(qo_b)
        x_recv = flip_z(x_own)
        gu_keep, gu_give = halves(gate_up, 1, core)
        gu_recv = flip_core(gu_give)
        mask = build_mask(columns, live_two, len(PIECES) * kv_rows // LANES)
        qo_a, qo_b, a_recv, b_recv, cross_k, side_k, own_v, x_own, x_recv, gu_keep, gu_recv, mask, down_w, down_recv = fence(
            qo_a, qo_b, a_recv, b_recv, cross_k, side_k, own_v, x_own, x_recv, gu_keep, gu_recv, mask, down_w, down_recv
        )

        cross_v, cross_side_k = cross(own_v), flip_x(cross_k)
        qo_a, qo_b = ordered(qo_a, a_recv, x, 2), ordered(qo_b, b_recv, y, 3)
        a_recv, b_recv = flip_y(qo_a), flip_x(qo_b)
        gu_keep, gu_give = halves(ordered(gu_keep, gu_recv, core, 2), 0, low)
        gu_recv = flip_z(gu_give)
        x_two = ordered(x_own[None], x_recv[None], low, 0)
        x_recv = flip_core(x_two)
        qo_a, qo_b, a_recv, b_recv, cross_v, cross_side_k, own_v, gu_keep, gu_recv, x_two, x_recv, mask, down_w, down_recv = fence(
            qo_a, qo_b, a_recv, b_recv, cross_v, cross_side_k, own_v, gu_keep, gu_recv, x_two, x_recv, mask, down_w, down_recv
        )

        cross_side_v, side_v = flip_x(cross_v), flip_x(own_v)
        other_mask = flip_core(mask)
        w_a, w_b = flat(ordered(qo_a, a_recv, y, 3)), flat(ordered(qo_b, b_recv, x, 2))
        gate_up = ordered(gu_keep[:, None], gu_recv[:, None], low, 1)[:, None]
        gu_recv = flip(gate_up, "seg", 4)
        down_w = ordered(down_w, down_recv, high, 0)
        down_recv = flip_y(down_w)
        x_all = jnp.stack([x_two, x_recv], 1).reshape(4, seg_len, width)
        queries, keys, values, h_one, inv_one = project(x_all, w_a, w_b, cosine, sine)
        wo_near = w_b[:, :quarter]
        queries, keys, values, cross_side_v, side_v, gate_up, gu_recv, down_w, down_recv, wo_near, g_own, other_mask = fence(
            queries, keys, values, cross_side_v, side_v, gate_up, gu_recv, down_w, down_recv, wo_near, g_own, other_mask
        )

        key_pieces = (cross_k, cross_side_k, side_k, own_k)
        value_pieces = (cross_v, cross_side_v, side_v, own_v)
        gate, upw = [ordered(gate_up[i], gu_recv[i], high, 0)[:, :, None, None] for i in range(2)]
        down_w = ordered(down_w, down_recv, y, 3)
        down_a, down_b = down_w[..., : width // 2], down_w[..., width // 2 :]
        g_recv, u_recv, a_recv, wo_far = flip_x(gate), flip_y(upw), flip_x(down_a), flip_z(wo_near)
        out_low, out_f32, p_memory, p_local, inverse = attention_forward(
            queries, keys, values, mask, other_mask, key_pieces, value_pieces
        )
        out_low, gate, upw, g_recv, u_recv, down_a, a_recv, down_b, wo_near, wo_far, g_own = fence(
            out_low, gate, upw, g_recv, u_recv, down_a, a_recv, down_b, wo_near, wo_far, g_own
        )
    else:
        qo = gather_high(ordered(qo_keep[None], qo_near[None], low, 0)[None, :, None, None])
        kv = ordered(kv_keep[:, None], kv_recv[:, None], low, 1)
        w_a, w_b = flat(gather_y(gather_x(qo[..., :split]))), flat(gather_x(gather_y(qo[..., split:])))
        x_all = all_blocks(two_rows(x_own))
        gu_keep, gu_give = halves(gate_up, 1, core)
        gu_keep, gu_give = halves(ordered(gu_keep, flip_core(gu_give), core, 2), 0, low)
        gate, upw = gather_high_pair(ordered(gu_keep[:, None], flip_z(gu_give)[:, None], low, 1))
        down_w = gather_y(gather_high(down_w))
        down_a, down_b = down_w[..., : width // 2], down_w[..., width // 2 :]
        coded = all_blocks(coded)
        row_core = jnp.bitwise_xor(core, jnp.arange(4, dtype=jnp.int32) % 2)[:, None, None]
        picks, slot_seg, within = places_of(coded, row_core)
        live_all = jnp.bitwise_and(coded[:, :, 0], 1)[:, None, :]
        columns = jnp.where(picks >= 0, slot_seg * kv_rows + within, n_seg * kv_rows)
        blocks_at = jnp.arange(4)[:, None, None]
        queries_at = jnp.arange(seg_len)[None, :, None]
        allow = jnp.zeros((4, seg_len, n_seg * kv_rows), BF).at[blocks_at, queries_at, columns].set(1.0, mode="drop")
        allow = allow.reshape(4, seg_len, n_seg, kv_rows).transpose(2, 0, 1, 3)
        memory = jnp.swapaxes(kv, 0, 1)[None, :, None]
        memory = gather_x(gather_high(memory)).reshape(n_seg, 2, kv_rows, quarter)
        queries, keys, values, h_one, inv_one = project(x_all, w_a, w_b, cosine, sine)
        wo_near = w_b[:, :quarter]
        out_low, out_f32, log_total = stream_forward(queries, keys, values, live_all, allow, memory)
        g_recv, u_recv, a_recv, wo_far = flip_x(gate), flip_y(upw), flip_x(down_a), flip_z(wo_near)

    h_one = h_one.reshape(group_tokens, width)
    inv_one = inv_one.reshape(group_tokens, 1)
    x_float = x_all.reshape(group_tokens, width).astype(F32)
    g_attn = w_b[:, quarter].astype(F32)
    g_ffn = w_b[:, quarter + 1].astype(F32)
    att_near = out_low.reshape(group_tokens, quarter)
    att_far = flip_z(att_near)
    gate, upw = ordered(gate, g_recv, x, 2), ordered(upw, u_recv, y, 3)
    g_recv, u_recv = flip_y(gate), flip_x(upw)
    wo_both = jnp.stack([wo_near, wo_far])
    wo_recv = flip_core(wo_both)
    g_far = flip_z(g_own)
    wo = join_four(wo_both, wo_recv, False)
    att_near, att_far, gate, upw, g_recv, u_recv, down_b, wo, g_own, g_far = fence(
        att_near, att_far, gate, upw, g_recv, u_recv, down_b, wo, g_own, g_far
    )

    att_both = jnp.stack([att_near, att_far])
    att_recv = flip_core(att_both)
    down_recv = flip_x(down_b)
    g_two = ordered(g_own[None], g_far[None], low, 0)
    g_recv_core = flip_core(g_two)
    wg, wu = flat(ordered(gate, g_recv, y, 3)), flat(ordered(upw, u_recv, x, 2))
    attended = join_four(att_both, att_recv, True)
    x_one = x_float + matmul(attended, wo)
    h_two_f, inv_two = norm_forward(x_one, g_ffn)
    h_two = h_two_f.astype(BF)
    gate_out = matmul(h_two, wg)
    up_out = matmul(h_two, wu)
    sigma = jax.nn.sigmoid(gate_out)
    swish = gate_out * sigma
    hidden = (swish * up_out).astype(BF)
    grad_out = jnp.stack([g_two, g_recv_core], 1).reshape(group_tokens, width)

    down_b, hidden = fence(down_b, hidden)
    wd = jnp.concatenate([flat(ordered(down_a, a_recv, x, 2)), flat(ordered(down_b, down_recv, x, 2))], 1)
    d_hidden = matmul_cols(grad_out, wd)
    d_gate = (d_hidden * up_out * sigma * (1.0 + gate_out * (1.0 - sigma))).astype(BF)
    d_up = (d_hidden * swish).astype(BF)
    sums_keep, sums_give = back_project([d_gate, d_up], [wg, wu])
    sums = add_low(sums_keep, flip_core(sums_give))
    sums, hidden, h_two, d_gate, d_up, wd = fence(sums, hidden, h_two, d_gate, d_up, wd)

    far_sums = flip_z(sums)
    (keep_g, give_g), (keep_u, give_u) = gradient((h_two, [d_gate], "x", None), (h_two, [d_up], "y", None))
    keep_g, give_g, keep_u, give_u, hidden, wd = fence(keep_g, give_g, keep_u, give_u, hidden, wd)
    recv_g, recv_u = flip_x(give_g), flip_y(give_u)
    down_keep, down_give = back_project([hidden], [wd], False)
    down_recv = flip_core(down_give)
    keep_wd, give_wd = gradient_units(hidden, grad_out)
    sums, far_sums, keep_g, keep_u, recv_g, recv_u, down_keep, down_recv, keep_wd, give_wd = fence(
        sums, far_sums, keep_g, keep_u, recv_g, recv_u, down_keep, down_recv, keep_wd, give_wd
    )

    own = 2 * low * seg_len
    summed = add_kernel(sums, far_sums)
    summed_recv = flip_core(summed)
    d_branch, d_att, d_x_own = branch_back(
        summed,
        summed_recv,
        x_one.reshape(4, seg_len, width),
        g_ffn[None],
        g_two,
        g_recv_core,
        wo,
    )
    d_branch = d_branch.reshape(group_tokens, width)
    keep_g, keep_u, recv_g, recv_u, d_att, d_branch, down_keep, down_recv = fence(
        keep_g, keep_u, recv_g, recv_u, d_att, d_branch, down_keep, down_recv
    )

    keep_g, give_g = split_sums(keep_g, recv_g, "y")
    keep_u, give_u = split_sums(keep_u, recv_u, "x")
    down_own, down_give = pair_add(down_keep, down_recv)
    w_thirds = [w_a[:, i * quarter : (i + 1) * quarter] for i in range(3)]
    if use_kernel:
        recv_g, recv_u = flip_y(give_g), flip_x(give_u)
        down_recv = flip_z(down_give)
        d_kv, dq_local = attention_backward_local(
            d_att, out_f32, queries, keys, values, inverse, p_local, cosine, sine
        )
        d_kv = d_kv.reshape(2, group_tokens, quarter)
        (keep_kv, give_kv), (keep_wo, give_wo) = gradient(
            (h_one, [d_kv[0], d_kv[1]], "y", None), (attended, [d_branch], "y", quarter)
        )
        give_kvo = jnp.concatenate([give_kv, give_wo], -1)
        keep_kvo = jnp.concatenate([keep_kv, keep_wo], -1)
        keep_kvo, give_kvo, keep_g, recv_g, keep_u, recv_u, dq_local, keep_wd, give_wd, down_own, down_recv = fence(
            keep_kvo, give_kvo, keep_g, recv_g, keep_u, recv_u, dq_local, keep_wd, give_wd, down_own, down_recv
        )
        gu_parts = plane_sort((keep_g, recv_g), (keep_u, recv_u))
        recv_kvo = flip_y(give_kvo)
        gu_flips = z_flips(gu_parts)
        recv_wd = flip_x(give_wd)
        d_q = attention_backward(
            d_att, out_f32, dq_local, inverse, p_memory, cosine, sine, key_pieces, value_pieces
        )
        d_q, keep_kvo = fence(d_q, keep_kvo)

        d_q = d_q.reshape(group_tokens, quarter)
        ((keep_q, *give_q),) = gradient((h_one, [d_q], "xy", None))
        keep_q, give_q, d_q, keep_kvo, recv_kvo, keep_wd, recv_wd, gu_kept, gu_flips = fence(
            keep_q, give_q, d_q, keep_kvo, recv_kvo, keep_wd, recv_wd, gu_parts[0], gu_flips
        )
        recv_q = plane_flips(give_q)
        keep_kvo, give_kvo = split_sums(keep_kvo, recv_kvo, "x")
        keep_wd, give_wd = split_sums(
            keep_wd.reshape((-1,) + keep_wd.shape[2:]), recv_wd.reshape((-1,) + keep_wd.shape[2:]), "y"
        )
        recv_wd = flip_y(give_wd)
        recv_kvo = flip_x(give_kvo)
        d_h_keep, d_h_give = back_project([d_q, d_kv[0], d_kv[1]], w_thirds)
        gu_keep, gu_give = z_merge(gu_kept, *gu_flips)
        keep_q, recv_q, keep_kvo, recv_kvo, keep_wd, recv_wd, d_h_keep, d_h_give, gu_keep, gu_give = fence(
            keep_q, recv_q, keep_kvo, recv_kvo, keep_wd, recv_wd, d_h_keep, d_h_give, gu_keep, gu_give
        )
        d_h_recv = flip_core(d_h_give)
        *parts, wd_own = plane_sort((keep_q,) + tuple(recv_q), (keep_kvo, recv_kvo), units=(keep_wd, recv_wd))
        flips = z_flips(parts)
        d_h_own, d_h_give = pair_add(d_h_keep, d_h_recv)
        d_h_recv = flip_z(d_h_give)
        gu_recv = flip_core(gu_give)
        sum_wg, sum_wu, grad_g_ffn = join_units(gu_keep, gu_recv, (w_gate, w_up), gain_ffn, n_devices)
        kept, flips, d_h_own, d_h_recv, wd_own, sum_wg, sum_wu = fence(
            parts[0], flips, d_h_own, d_h_recv, wd_own, sum_wg, sum_wu
        )
        qkvo_keep, qkvo_give = z_merge(kept, *flips)
        qkvo_recv = flip_core(qkvo_give)
        wd_recv = flips[1][kept.shape[0] : kept.shape[0] + wd_own.shape[0]]
        sum_wd = wd_own.astype(F32) + wd_recv.astype(F32)
    else:
        down_recv = flip_z(down_give)
        recv_wd = flip_x(give_wd)
        d_q, *d_kv = stream_backward(
            d_att, out_f32, queries, keys, values, live_all, log_total, allow, memory, cosine, sine
        ).reshape(3, group_tokens, quarter)

        def by_chip(value):
            return value.reshape(n_high, 2, -1, value.shape[-1])

        (keep_qkv, *give_qkv), (keep_wo, *give_wo) = gradient(
            (h_one, [d_q, d_kv[0], d_kv[1]], "xy", None), (attended, [d_branch], "xy", quarter)
        )
        plane_gu = [add_low(keep_g, flip_y(give_g)), add_low(keep_u, flip_x(give_u))]
        z_gu = z_plain(by_chip(jnp.concatenate(plane_gu, -1)))
        plane_qkvo = [add_all(keep_qkv, *plane_flips(give_qkv)), add_all(keep_wo, *plane_flips(give_wo))]
        z_qkvo = z_plain(by_chip(jnp.concatenate(plane_qkvo, -1)))
        (gu_keep, gu_give), (qkvo_keep, qkvo_give) = core_halves(z_gu), core_halves(z_qkvo)
        qkvo_recv, gu_recv = flip_core(qkvo_give), flip_core(gu_give)
        keep_wd, give_wd = halves(add_low(keep_wd, recv_wd), 1, y)
        recv_wd = flip_y(give_wd)
        d_h_keep, d_h_give = back_project([d_q, d_kv[0], d_kv[1]], w_thirds)
        d_h_own, d_h_give = pair_add(d_h_keep, flip_core(d_h_give))
        d_h_recv = flip_z(d_h_give)
        sum_wd = reduce_high(add_low(keep_wd, recv_wd)[:, None])[0].astype(F32)
        sum_wg, sum_wu, grad_g_ffn = join_units(gu_keep, gu_recv, (w_gate, w_up), gain_ffn, n_devices)
    layer_output = (cut(x_one, own, seg_len, 0) + down_own.astype(F32) + down_recv.astype(F32)).astype(BF)
    sum_q, sum_k, sum_v, sum_o, grad_g_attn = join_columns(
        qkvo_keep, qkvo_recv, (w_query, w_key, w_value), gain_attn, 4
    )
    d_h_one = d_h_own.astype(F32) + d_h_recv.astype(F32)
    x_own = cut(x_float, own, seg_len, 0)
    d_x_first, unused = norm_backward(x_own, cut(inv_one, own, seg_len, 0), g_attn, d_h_one)
    grad_x = (d_x_own + d_x_first).astype(BF)
    return (
        layer_output[None],
        grad_x[None],
        grad_g_attn,
        sum_q,
        sum_k,
        sum_v,
        sum_o,
        grad_g_ffn,
        sum_wg,
        sum_wu,
        sum_wd,
    )


def solution(mesh):
    tokens = P("rep", "seg", None)
    vector = P(("seg", "rep"))
    matrix = P(("seg", "rep"), None)
    return jax.shard_map(
        local,
        mesh=mesh,
        in_specs=(
            tokens,
            P("rep", "seg"),
            tokens,
            tokens,
            tokens,
            vector,
            matrix,
            matrix,
            matrix,
            matrix,
            vector,
            matrix,
            matrix,
            matrix,
            tokens,
        ),
        out_specs=(tokens, tokens, vector, matrix, matrix, matrix, matrix, vector, matrix, matrix, matrix),
        check_vma=False,
    )
```

profile of v0, /device:TPU:0, one launch (start us, length us, event | category | flops | bytes accessed | tf_op | source)
XLA Modules:
  0.0 317.5 jit_solution(16088451085458699930)
XLA Ops:
  18.8 6.8 %collective-permute-done.7 = bf16[1,1,1,1,88,1024]{5,4,3,2,1,0:T(8,128)(2,1)S(1)} collective-permute-done((bf16[1,1,1,1,88,1024]{5,4,3,2,1,0:T(8,128)(2,1)S(1)}, bf16[1,1,1,1,88,1024]{5,4,3,2,1,0:T(8,128)(2,1)S(1)}, u32[]{:S(2)}, u32[]{:S(2)}) %collective-permute-start.7) | collective-permute-done | bytes 180256 | tf_op jit(solution)/shard_map/ppermute | solution.py:30
  26.0 6.3 %collective-permute-done.4 = bf16[64,1152]{1,0:T(8,128)(2,1)S(1)} collective-permute-done((bf16[64,1152]{1,0:T(8,128)(2,1)S(1)}, bf16[64,1152]{1,0:T(8,128)(2,1)S(1)}, u32[]{:S(2)}, u32[]{:S(2)}) %collective-permute-start.4) | collective-permute-done | bytes 147488 | tf_op jit(solution)/shard_map/ppermute | solution.py:30
  32.3 4.0 %collective-permute-done.6 = bf16[2,384,256]{2,1,0:T(8,128)(2,1)S(1)} collective-permute-done((bf16[2,384,256]{2,1,0:T(8,128)(2,1)S(1)}, bf16[2,384,256]{2,1,0:T(8,128)(2,1)S(1)}, u32[]{:S(2)}, u32[]{:S(2)}) %collective-permute-start.6) | collective-permute-done | bytes 393248 | tf_op jit(solution)/shard_map/ppermute | solution.py:30
  47.2 10.6 %mask_build.1.mine_ref = bf16[2,23,192,128]{3,2,1,0:T(8,128)(2,1)S(1)} custom-call(s32[2,192,128]{2,1,0:T(8,128)S(1)} %copy.84.refs_0_, s32[2,1,256]{2,1,0:T(1,128)S(1)} %pad.4.refs_1_), custom_call_target="tpu_custom_call" | custom-call | flops 12000000000 | bytes 3000000 | tf_op jit(solution)/shard_map/mask_build/pallas_call | solution.py:313
  66.4 5.7 %collective-permute-start.16 = (bf16[2,384,256]{2,1,0:T(8,128)(2,1)S(1)}, bf16[2,384,256]{2,1,0:T(8,128)(2,1)S(1)}, u32[]{:S(2)}, u32[]{:S(2)}) collective-permute-start(bf16[2,384,256]{2,1,0:T(8,128)(2,1)S(1)} %get-tuple-element.282.refs_7_), channel_id=1, source_target_pairs={{0,16},{4,20},{8,24},{12,28},{1,17},{5,21},{9,25},{13,29},{2,18},{... | collective-permute-start | bytes 1179656 | tf_op jit(solution)/shard_map/ppermute | solution.py:1196
  72.8 5.1 %collective-permute-done.15 = bf16[2,2,1,2,64,384]{5,4,3,2,1,0:T(8,128)(2,1)S(1)} collective-permute-done((bf16[2,2,1,2,64,384]{5,4,3,2,1,0:T(8,128)(2,1)S(1)}, bf16[2,2,1,2,64,384]{5,4,3,2,1,0:T(8,128)(2,1)S(1)}, u32[]{:S(2)}, u32[]{:S(2)}) %collective-permute-start.15) | collective-permute-done | bytes 393248 | tf_op jit(solution)/shard_map/ppermute | solution.py:30
  80.2 5.1 %collective-permute-done.17.refs_1_ = bf16[2,384,256]{2,1,0:T(8,128)(2,1)S(1)} collective-permute-done((bf16[2,384,256]{2,1,0:T(8,128)(2,1)S(1)}, bf16[2,384,256]{2,1,0:T(8,128)(2,1)S(1)}, u32[]{:S(2)}, u32[]{:S(2)}) %collective-permute-start.17) | collective-permute-done | bytes 393248 | tf_op jit(solution)/shard_map/ppermute | solution.py:30
  86.7 3.8 %collective-permute-start.22 = (bf16[2,1,2,64,704]{4,3,2,1,0:T(8,128)(2,1)S(1)}, bf16[2,1,2,64,704]{4,3,2,1,0:T(8,128)(2,1)S(1)}, u32[]{:S(2)}, u32[]{:S(2)}) collective-permute-start(bf16[2,1,2,64,704]{4,3,2,1,0:T(8,128)(2,1)S(1)} %maximum_bitcast_fusion.1), channel_id=1, source_target_pairs={{0,16},{4,20},{8,24},{12,28},{16,0},{20,4},{24,8},{28,12},{1,17},{... | collective-permute-start | bytes 1081352 | tf_op jit(solution)/shard_map/ppermute | solution.py:30
  97.9 10.5 %collective-permute-done.22 = bf16[2,1,2,64,704]{4,3,2,1,0:T(8,128)(2,1)S(1)} collective-permute-done((bf16[2,1,2,64,704]{4,3,2,1,0:T(8,128)(2,1)S(1)}, bf16[2,1,2,64,704]{4,3,2,1,0:T(8,128)(2,1)S(1)}, u32[]{:S(2)}, u32[]{:S(2)}) %collective-permute-start.22) | collective-permute-done | bytes 360480 | tf_op jit(solution)/shard_map/ppermute | solution.py:30
  109.9 4.3 %collective-permute-start.28 = (bf16[1024,256]{1,0:T(8,128)(2,1)S(1)}, bf16[1024,256]{1,0:T(8,128)(2,1)S(1)}, u32[]{:S(2)}, u32[]{:S(2)}) collective-permute-start(bf16[1024,256]{1,0:T(8,128)(2,1)S(1)} %slice.154), channel_id=1, source_target_pairs={{0,8},{4,12},{8,0},{12,4},{16,24},{20,28},{24,16},{28,20},{1,9},{5... | collective-permute-start | bytes 1572872 | tf_op jit(solution)/shard_map/ppermute | solution.py:30
  118.1 15.5 %attention_forward.1 = (bf16[4,192,256]{2,1,0:T(8,128)(2,1)S(1)}, f32[4,192,256]{2,1,0:T(8,128)S(1)}, bf16[4,2,7,192,384]{4,3,2,1,0:T(8,128)(2,1)}, bf16[4,2,192...) custom-call(bf16[4,192,256]{2,1,0:T(8,128)(2,1)S(1)} %get-tuple-element.288.q_ref, ...), custom_call_target="tpu_custom_call" | custom-call | flops 1000 | bytes 1000 | tf_op jit(solution)/shard_map/attention_forward/pallas_call | solution.py:950
  141.1 4.1 %copy.85 = f32[2,2,192,1024]{3,2,1,0:T(8,128)} copy(f32[2,2,192,1024]{3,2,0,1:T(8,128)} %get-tuple-element.478) | data formatting | bytes 6291456 | tf_op jit(solution)/shard_map/convert_element_type | solution.py:1273
  147.3 3.7 %collective-permute-done.29 = bf16[768,256]{1,0:T(8,128)(2,1)S(1)} collective-permute-done((bf16[768,256]{1,0:T(8,128)(2,1)}, bf16[768,256]{1,0:T(8,128)(2,1)S(1)}, u32[]{:S(2)}, u32[]{:S(2)}) %collective-permute-start.29) | collective-permute-done | bytes 393248 | tf_op jit(solution)/shard_map/ppermute | solution.py:30
  151.0 7.7 %collective-permute-done.33 = bf16[192,1024]{1,0:T(8,128)(2,1)S(1)} collective-permute-done((bf16[192,1024]{1,0:T(8,128)(2,1)}, bf16[192,1024]{1,0:T(8,128)(2,1)S(1)}, u32[]{:S(2)}, u32[]{:S(2)}) %collective-permute-start.33) | collective-permute-done | bytes 393248 | tf_op jit(solution)/shard_map/ppermute | solution.py:30
  166.6 4.4 %multiply_reduce_fusion = (f32[768]{0:T(1024)S(1)}, f32[768,1024]{1,0:T(8,128)S(1)}) fusion(f32[768,1024]{1,0:T(8,128)} %bitcast.172, bf16[768,1024]{1,0:T(8,128)(2,1)S(1)} %join_four.3.refs_1_, bf16[1024,1024]{1,0:T(8,128)(2,1)S(1)} %join_four.2.w_ref), kind=kOutput, calls=%fused_computation.1 | convolution fusion | flops 1612971264 | bytes 9964544 | tf_op jit(solution)/shard_map/dot_general | solution.py:250
  178.7 3.5 %back_project.3 = (bf16[2,192,1024]{2,1,0:T(8,128)(2,1)S(1)}, bf16[2,192,1024]{2,1,0:T(8,128)(2,1)}) custom-call(bf16[768,704]{1,0:T(8,128)(2,1)S(1)} %get-tuple-element.331.refs_0_.refs_1_, bf16[768,704]{1,0:T(8,128)(2,1)S(1)} %get-tuple-element.332.refs_1_.refs_2_, bf16[1024,704]{1,0:T(8,128)(2,1)S(1)} %bitcast.152, bf16[1024,704]{1,0:T(8,128)(2,1)S(1)} %bitcast.154), custom_call_target="tpu_custom_call" | custom-call | flops 1000 | bytes 1000 | tf_op jit(solution)/shard_map/back_project/pallas_call | solution.py:697
  187.4 5.0 %gradient.3 = (bf16[8,64,704]{2,1,0:T(8,128)(2,1)S(1)}, bf16[8,64,704]{2,1,0:T(8,128)(2,1)}, bf16[8,64,704]{2,1,0:T(8,128)(2,1)S(1)}, bf16[8,64,704]{2,1,0:T(8,128)(2,1)S(1)}) custom-call(s32[3]{0:T(128)S(1)} %pad_add_fusion.2.at_ref, bf16[768,1024]{1,0:T(8,128)(2,1)S(1)} %copy-done.7, bf16[768,704]{1,0:T(8,128)(2,1)S(1)} %copy-done.12, ...), custom_call_target="tpu_custom_call" | custom-call | flops 1000 | bytes 1000 | tf_op jit(solution)/shard_map/gradient/pallas_call | solution.py:448
  199.2 15.0 %collective-permute-done.39.recv_ref = bf16[8,64,704]{2,1,0:T(8,128)(2,1)S(1)} collective-permute-done((bf16[8,64,704]{2,1,0:T(8,128)(2,1)}, bf16[8,64,704]{2,1,0:T(8,128)(2,1)S(1)}, u32[]{:S(2)}, u32[]{:S(2)}) %collective-permute-start.39) | collective-permute-done | bytes 720928 | tf_op jit(solution)/shard_map/ppermute | solution.py:30
  216.9 4.8 %branch_back.1 = (bf16[4,192,1024]{2,1,0:T(8,128)(2,1)S(1)}, bf16[4,192,256]{2,1,0:T(8,128)(2,1)S(1)}, f32[192,1024]{1,0:T(8,128)S(1)}) custom-call(s32[3]{0:T(128)S(1)} %pad_add_fusion.1.at_ref, bf16[2,192,1024]{2,1,0:T(8,128)(2,1)S(1)} %add_kernel.1.mine_ref, bf16[2,192,1024]{2,1,0:T(8,128)(2,1)S(1)} %collective-permute-done.42.recv_ref, ...), custom_call_target="tpu_custom_call" | custom-call | flops 1000 | bytes 1000 | tf_op jit(solution)/shard_map/branch_back/pallas_call | solution.py:759
  228.1 5.0 %attention_backward_local.1 = (bf16[2,4,192,256]{3,2,1,0:T(8,128)(2,1)S(1)}, f32[4,192,256]{2,1,0:T(8,128)S(1)}) custom-call(bf16[4,192,256]{2,1,0:T(8,128)(2,1)S(1)} %get-tuple-element.359.do_ref, f32[4,192,256]{2,1,0:T(8,128)S(1)} %copy-done.18, bf16[4,192,256]{2,1,0:T(8,128)(2,1)S(1)} %copy-done.42, bf16[4,192,256]{2,1,0:T(8,128)(2,1)S(1)} %copy-done.44, ...), custom_call_target="tpu_custom_call" | custom-call | flops 1000 | bytes 1000 | tf_op jit(solution)/shard_map/attention_backward_local/pallas_call | solution.py:985
  242.0 3.5 %collective-permute-start.50 = (bf16[64,1408]{1,0:T(8,128)(2,1)S(1)}, bf16[64,1408]{1,0:T(8,128)(2,1)S(1)}, u32[]{:S(2)}, u32[]{:S(2)}) collective-permute-start(bf16[64,1408]{1,0:T(8,128)(2,1)S(1)} %get-tuple-element.407), channel_id=1, source_target_pairs={{0,24},{4,28},{8,16},{12,20},{16,8},{20,12},{24,0},{28,4},{1,25},{... | collective-permute-start | bytes 540680 | tf_op jit(solution)/shard_map/ppermute | solution.py:30
  245.5 12.4 %attention_backward.1 = bf16[4,192,256]{2,1,0:T(8,128)(2,1)S(1)} custom-call(bf16[4,192,256]{2,1,0:T(8,128)(2,1)S(1)} %get-tuple-element.359.do_ref, f32[4,192,256]{2,1,0:T(8,128)S(1)} %copy-done.18, f32[4,192,256]{2,1,0:T(8,128)S(1)} %get-tuple-element.388.local_ref, f32[4,2,192,1]{3,2,1,0:T(8,128)S(1)} %copy-done.20, ...), custom_call_target="tpu_custom_call" | custom-call | flops 1000 | bytes 1000 | tf_op jit(solution)/shard_map/attention_backward/pallas_call | solution.py:1006
  297.7 3.9 %collective-permute-done.56.one_ref = bf16[64,1024]{1,0:T(8,128)(2,1)S(1)} collective-permute-done((bf16[64,1024]{1,0:T(8,128)(2,1)}, bf16[64,1024]{1,0:T(8,128)(2,1)S(1)}, u32[]{:S(2)}, u32[]{:S(2)}) %collective-permute-start.56) | collective-permute-done | bytes 131104 | tf_op jit(solution)/shard_map/ppermute | solution.py:30
  301.6 3.4 %collective-permute-done.58.three_ref = bf16[64,1024]{1,0:T(8,128)(2,1)S(1)} collective-permute-done((bf16[64,1024]{1,0:T(8,128)(2,1)}, bf16[64,1024]{1,0:T(8,128)(2,1)S(1)}, u32[]{:S(2)}, u32[]{:S(2)}) %collective-permute-start.58) | collective-permute-done | bytes 131104 | tf_op jit(solution)/shard_map/ppermute | solution.py:30
  (454 shorter events, 160.7 us)
Async XLA Ops:
  12.8 19.5 %collective-permute-start.4 = (bf16[64,1152]{1,0:T(8,128)(2,1)S(1)}, bf16[64,1152]{1,0:T(8,128)(2,1)S(1)}, u32[]{:S(2)}, u32[]{:S(2)}) collective-permute-start(bf16[64,1152]{1,0:T(8,128)(2,1)S(1)} %get-tuple-element.247), channel_id=1, source_target_pairs={{0,16},{4,20},{8,24},{12,28},{16,0},{20,4},{24,8},{28,12},{1,17},{... | collective-permute-start | bytes 442376 | tf_op jit(solution)/shard_map/ppermute | solution.py:30
  15.8 20.5 %collective-permute-start.6 = (bf16[2,384,256]{2,1,0:T(8,128)(2,1)S(1)}, bf16[2,384,256]{2,1,0:T(8,128)(2,1)S(1)}, u32[]{:S(2)}, u32[]{:S(2)}) collective-permute-start(bf16[2,384,256]{2,1,0:T(8,128)(2,1)S(1)} %get-tuple-element.506), channel_id=1, source_target_pairs={{0,8},{4,12},{8,0},{12,4},{16,24},{20,28},{24,16},{28,20},{1,9},{5... | collective-permute-start | bytes 1179656 | tf_op jit(solution)/shard_map/ppermute | solution.py:30
  39.3 20.4 %collective-permute-start.11 = (bf16[2,384,256]{2,1,0:T(8,128)(2,1)S(1)}, bf16[2,384,256]{2,1,0:T(8,128)(2,1)S(1)}, u32[]{:S(2)}, u32[]{:S(2)}) collective-permute-start(bf16[2,384,256]{2,1,0:T(8,128)(2,1)S(1)} %get-tuple-element.503.refs_3_), channel_id=1, source_target_pairs={{0,4},{4,0},{8,12},{12,8},{16,20},{20,16},{24,28},{28,24},{1,5},{5... | collective-permute-start | bytes 1179656 | tf_op jit(solution)/shard_map/ppermute | solution.py:30
  40.8 18.9 %collective-permute-start.10 = (bf16[2,384,256]{2,1,0:T(8,128)(2,1)S(1)}, bf16[2,384,256]{2,1,0:T(8,128)(2,1)S(1)}, u32[]{:S(2)}, u32[]{:S(2)}) collective-permute-start(bf16[2,384,256]{2,1,0:T(8,128)(2,1)S(1)} %get-tuple-element.503.refs_3_), channel_id=1, source_target_pairs={{0,16},{4,20},{8,24},{12,28},{1,17},{5,21},{9,25},{13,29},{2,18},{... | collective-permute-start | bytes 1179656 | tf_op jit(solution)/shard_map/ppermute | solution.py:1196
  60.5 24.8 %collective-permute-start.19 = (bf16[2,192,1024]{2,1,0:T(8,128)(2,1)S(1)}, bf16[2,192,1024]{2,1,0:T(8,128)(2,1)S(1)}, u32[]{:S(2)}, u32[]{:S(2)}) collective-permute-start(bf16[2,192,1024]{2,1,0:T(8,128)(2,1)S(1)} %pad_maximum_fusion.8), channel_id=1, source_target_pairs={{0,1},{1,0},{2,3},{3,2},{4,5},{5,4},{6,7},{7,6},{8,9},{9,8},{10,11... | collective-permute-start | bytes 2359304 | tf_op jit(solution)/shard_map/ppermute | solution.py:30
  60.6 24.6 %collective-permute-start.14 = (bf16[2,2,2,1,64,768]{5,4,3,2,1,0:T(8,128)(2,1)S(1)}, bf16[2,2,2,1,64,768]{5,4,3,2,1,0:T(8,128)(2,1)S(1)}, u32[]{:S(2)}, u32[]{:S(2)}) collective-permute-start(bf16[2,2,2,1,64,768]{5,4,3,2,1,0:T(8,128)(2,1)S(1)} %pad_maximum_fusion.7), channel_id=1, source_target_pairs={{0,2},{1,3},{2,0},{3,1},{4,6},{5,7},{6,4},{7,5},{8,10},{9,11},{10,... | collective-permute-start | bytes 2359304 | tf_op jit(solution)/shard_map/ppermute | solution.py:30
  85.3 24.6 %collective-permute-start.24 = (bf16[2,23,192,128]{3,2,1,0:T(8,128)(2,1)S(1)}, bf16[2,23,192,128]{3,2,1,0:T(8,128)(2,1)S(1)}, u32[]{:S(2)}, u32[]{:S(2)}) collective-permute-start(bf16[2,23,192,128]{3,2,1,0:T(8,128)(2,1)S(1)} %mask_build.1.mine_ref), channel_id=1, source_target_pairs={{0,1},{1,0},{2,3},{3,2},{4,5},{5,4},{6,7},{7,6},{8,9},{9,8},{10,11... | collective-permute-start | bytes 6782984 | tf_op jit(solution)/shard_map/ppermute | solution.py:30
  86.7 21.7 %collective-permute-start.22 = (bf16[2,1,2,64,704]{4,3,2,1,0:T(8,128)(2,1)S(1)}, bf16[2,1,2,64,704]{4,3,2,1,0:T(8,128)(2,1)S(1)}, u32[]{:S(2)}, u32[]{:S(2)}) collective-permute-start(bf16[2,1,2,64,704]{4,3,2,1,0:T(8,128)(2,1)S(1)} %maximum_bitcast_fusion.1), channel_id=1, source_target_pairs={{0,16},{4,20},{8,24},{12,28},{16,0},{20,4},{24,8},{28,12},{1,17},{... | collective-permute-start | bytes 1081352 | tf_op jit(solution)/shard_map/ppermute | solution.py:30
  109.9 23.8 %collective-permute-start.28 = (bf16[1024,256]{1,0:T(8,128)(2,1)S(1)}, bf16[1024,256]{1,0:T(8,128)(2,1)S(1)}, u32[]{:S(2)}, u32[]{:S(2)}) collective-permute-start(bf16[1024,256]{1,0:T(8,128)(2,1)S(1)} %slice.154), channel_id=1, source_target_pairs={{0,8},{4,12},{8,0},{12,4},{16,24},{20,28},{24,16},{28,20},{1,9},{5... | collective-permute-start | bytes 1572872 | tf_op jit(solution)/shard_map/ppermute | solution.py:30
  115.1 18.5 %collective-permute-start.27 = (bf16[2,1,1,2,88,512]{5,4,3,2,1,0:T(8,128)(2,1)S(1)}, bf16[2,1,1,2,88,512]{5,4,3,2,1,0:T(8,128)(2,1)S(1)}, u32[]{:S(2)}, u32[]{:S(2)}) collective-permute-start(bf16[2,1,1,2,88,512]{5,4,3,2,1,0:T(8,128)(2,1)S(1)} %get-tuple-element.318), channel_id=1, source_target_pairs={{0,4},{4,0},{8,12},{12,8},{16,20},{20,16},{24,28},{28,24},{1,5},{5... | collective-permute-start | bytes 1081352 | tf_op jit(solution)/shard_map/ppermute | solution.py:30
  135.4 23.3 %collective-permute-start.31 = (bf16[2,2,1,2,64,704]{5,4,3,2,1,0:T(8,128)(2,1)}, bf16[2,2,1,2,64,704]{5,4,3,2,1,0:T(8,128)(2,1)}, u32[]{:S(2)}, u32[]{:S(2)}) collective-permute-start(bf16[2,2,1,2,64,704]{5,4,3,2,1,0:T(8,128)(2,1)} %pad_maximum_fusion.11), channel_id=1, source_target_pairs={{0,4},{4,0},{8,12},{12,8},{16,20},{20,16},{24,28},{28,24},{1,5},{5... | collective-permute-start | bytes 2162696 | tf_op jit(solution)/shard_map/ppermute | solution.py:30
  137.2 21.4 %collective-permute-start.30 = (bf16[2,2,2,1,64,704]{5,4,1,0,3,2:T(8,128)(2,1)}, bf16[2,2,2,1,64,704]{5,4,1,0,3,2:T(8,128)(2,1)}, u32[]{:S(2)}, u32[]{:S(2)}) collective-permute-start(bf16[2,2,2,1,64,704]{5,4,1,0,3,2:T(8,128)(2,1)} %pad_maximum_fusion.10), channel_id=1, source_target_pairs={{0,2},{1,3},{2,0},{3,1},{4,6},{5,7},{6,4},{7,5},{8,10},{9,11},{10,... | collective-permute-start | bytes 2162696 | tf_op jit(solution)/shard_map/ppermute | solution.py:30
  139.0 19.6 %collective-permute-start.33 = (bf16[192,1024]{1,0:T(8,128)(2,1)}, bf16[192,1024]{1,0:T(8,128)(2,1)S(1)}, u32[]{:S(2)}, u32[]{:S(2)}) collective-permute-start(bf16[192,1024]{1,0:T(8,128)(2,1)} %bitcast.187), channel_id=1, source_target_pairs={{0,8},{4,12},{8,0},{12,4},{16,24},{20,28},{24,16},{28,20},{1,9},{5... | collective-permute-start | bytes 1179656 | tf_op jit(solution)/shard_map/ppermute | solution.py:30
  192.3 22.1 %collective-permute-start.38 = (bf16[2,192,1024]{2,1,0:T(8,128)(2,1)S(1)}, bf16[2,192,1024]{2,1,0:T(8,128)(2,1)S(1)}, u32[]{:S(2)}, u32[]{:S(2)}) collective-permute-start(bf16[2,192,1024]{2,1,0:T(8,128)(2,1)S(1)} %add_convert_fusion.one_ref), channel_id=1, source_target_pairs={{0,8},{4,12},{8,0},{12,4},{16,24},{20,28},{24,16},{28,20},{1,9},{5... | collective-permute-start | bytes 2359304 | tf_op jit(solution)/shard_map/ppermute | solution.py:30
  194.0 20.4 %collective-permute-start.41 = (bf16[2,192,1024]{2,1,0:T(8,128)(2,1)S(1)}, bf16[2,192,1024]{2,1,0:T(8,128)(2,1)S(1)}, u32[]{:S(2)}, u32[]{:S(2)}) collective-permute-start(bf16[2,192,1024]{2,1,0:T(8,128)(2,1)S(1)} %get-tuple-element.346), channel_id=1, source_target_pairs={{0,1},{1,0},{2,3},{3,2},{4,5},{5,4},{6,7},{7,6},{8,9},{9,8},{10,11... | collective-permute-start | bytes 2359304 | tf_op jit(solution)/shard_map/ppermute | solution.py:30
  194.2 20.1 %collective-permute-start.39 = (bf16[8,64,704]{2,1,0:T(8,128)(2,1)}, bf16[8,64,704]{2,1,0:T(8,128)(2,1)S(1)}, u32[]{:S(2)}, u32[]{:S(2)}) collective-permute-start(bf16[8,64,704]{2,1,0:T(8,128)(2,1)} %get-tuple-element.341), channel_id=1, source_target_pairs={{0,4},{4,0},{8,12},{12,8},{16,20},{20,16},{24,28},{28,24},{1,5},{5... | collective-permute-start | bytes 2162696 | tf_op jit(solution)/shard_map/ppermute | solution.py:30
  194.8 19.6 %collective-permute-start.40 = (bf16[8,64,704]{2,1,0:T(8,128)(2,1)S(1)}, bf16[8,64,704]{2,1,0:T(8,128)(2,1)S(1)}, u32[]{:S(2)}, u32[]{:S(2)}) collective-permute-start(bf16[8,64,704]{2,1,0:T(8,128)(2,1)S(1)} %get-tuple-element.342), channel_id=1, source_target_pairs={{0,2},{1,3},{2,0},{3,1},{4,6},{5,7},{6,4},{7,5},{8,10},{9,11},{10,... | collective-permute-start | bytes 2162696 | tf_op jit(solution)/shard_map/ppermute | solution.py:30
  238.0 22.9 %collective-permute-start.46 = (bf16[8,64,768]{2,1,0:T(8,128)(2,1)S(1)}, bf16[8,64,768]{2,1,0:T(8,128)(2,1)S(1)}, u32[]{:S(2)}, u32[]{:S(2)}) collective-permute-start(bf16[8,64,768]{2,1,0:T(8,128)(2,1)S(1)} %pad_maximum_fusion.15), channel_id=1, source_target_pairs={{0,2},{1,3},{2,0},{3,1},{4,6},{5,7},{6,4},{7,5},{8,10},{9,11},{10,... | collective-permute-start | bytes 2359304 | tf_op jit(solution)/shard_map/ppermute | solution.py:30
  239.6 21.4 %collective-permute-start.47 = (bf16[2,2,88,1024]{3,2,1,0:T(8,128)(2,1)S(1)}, bf16[2,2,88,1024]{3,2,1,0:T(8,128)(2,1)S(1)}, u32[]{:S(2)}, u32[]{:S(2)}) collective-permute-start(bf16[2,2,88,1024]{3,2,1,0:T(8,128)(2,1)S(1)} %copy-done.74), channel_id=1, source_target_pairs={{0,4},{4,0},{8,12},{12,8},{16,20},{20,16},{24,28},{28,24},{1,5},{5... | collective-permute-start | bytes 2162696 | tf_op jit(solution)/shard_map/ppermute | solution.py:30
  241.0 20.0 %collective-permute-start.48 = (bf16[64,1408]{1,0:T(8,128)(2,1)S(1)}, bf16[64,1408]{1,0:T(8,128)(2,1)S(1)}, u32[]{:S(2)}, u32[]{:S(2)}) collective-permute-start(bf16[64,1408]{1,0:T(8,128)(2,1)S(1)} %get-tuple-element.405), channel_id=1, source_target_pairs={{0,8},{4,12},{8,0},{12,4},{16,24},{20,28},{24,16},{28,20},{1,9},{5... | collective-permute-start | bytes 540680 | tf_op jit(solution)/shard_map/ppermute | solution.py:30
  241.6 19.4 %collective-permute-start.49 = (bf16[64,1408]{1,0:T(8,128)(2,1)S(1)}, bf16[64,1408]{1,0:T(8,128)(2,1)S(1)}, u32[]{:S(2)}, u32[]{:S(2)}) collective-permute-start(bf16[64,1408]{1,0:T(8,128)(2,1)S(1)} %get-tuple-element.406), channel_id=1, source_target_pairs={{0,16},{4,20},{8,24},{12,28},{16,0},{20,4},{24,8},{28,12},{1,17},{... | collective-permute-start | bytes 540680 | tf_op jit(solution)/shard_map/ppermute | solution.py:30
  242.0 19.0 %collective-permute-start.50 = (bf16[64,1408]{1,0:T(8,128)(2,1)S(1)}, bf16[64,1408]{1,0:T(8,128)(2,1)S(1)}, u32[]{:S(2)}, u32[]{:S(2)}) collective-permute-start(bf16[64,1408]{1,0:T(8,128)(2,1)S(1)} %get-tuple-element.407), channel_id=1, source_target_pairs={{0,24},{4,28},{8,16},{12,20},{16,8},{20,12},{24,0},{28,4},{1,25},{... | collective-permute-start | bytes 540680 | tf_op jit(solution)/shard_map/ppermute | solution.py:30
  282.0 26.3 %collective-permute-start.60 = (bf16[192,1024]{1,0:T(8,128)(2,1)}, bf16[192,1024]{1,0:T(8,128)(2,1)}, u32[]{:S(2)}, u32[]{:S(2)}) collective-permute-start(bf16[192,1024]{1,0:T(8,128)(2,1)} %get-tuple-element.444), channel_id=1, source_target_pairs={{0,8},{4,12},{8,0},{12,4},{16,24},{20,28},{24,16},{28,20},{1,9},{5... | collective-permute-start | bytes 1179656 | tf_op jit(solution)/shard_map/ppermute | solution.py:30
  286.7 21.5 %collective-permute-start.57 = (bf16[160,1024]{1,0:T(8,128)(2,1)}, bf16[160,1024]{1,0:T(8,128)(2,1)S(1)}, u32[]{:S(2)}, u32[]{:S(2)}) collective-permute-start(bf16[160,1024]{1,0:T(8,128)(2,1)} %get-tuple-element.439), channel_id=1, source_target_pairs={{0,16},{4,20},{8,24},{12,28},{16,0},{20,4},{24,8},{28,12},{1,17},{... | collective-permute-start | bytes 983048 | tf_op jit(solution)/shard_map/ppermute | solution.py:30
  (143 other events, 1534.7 us)
where the time goes:
time: 319 us; the launch traced here: 317 us
  waiting for transfers between devices  91.8 us (29%)
  Pallas kernels  89.1 us (28%)
  starting transfers between devices  72 us (23%)
  other arithmetic  27.4 us (9%)
  local copies, waits for them, and re-layouts  24.3 us (8%)
  matrix products  10.3 us (3%)
    ppermute x60, waiting for transfers between devices, flip(): return lax.ppermute(value, axis, [(i, i ^ bit) for i in range(count)])  89.5 us
    ppermute x60, starting transfers between devices, flip(): return lax.ppermute(value, axis, [(i, i ^ bit) for i in range(count)])  63.1 us
    pallas_call x1, Pallas kernels, attention_forward(): pl.pallas_call(forward_kernel, grid=(heads, blocks), in_specs=[head, head...  15.5 us
    unnamed x209, local copies, waits for them, and re-layouts  13.4 us
    pallas_call x1, Pallas kernels, attention_backward(): pl.pallas_call(backward_kernel, grid=(heads, blocks), in_specs=[head, hea...  12.4 us
    pallas_call x1, Pallas kernels, build_mask(): pl.pallas_call(lambda *refs: mask_kernel(n_cols, *refs), grid=(rows, quer...  10.6 us
    pallas_call x3, Pallas kernels, gradient(): pl.pallas_call(body, grid_spec=pltpu.PrefetchScalarGridSpec(num_scalar_pr...  10.5 us
    dot_general x3, matrix products, matmul(): return jnp.dot(left, right, preferred_element_type=F32)  8.36 us
  transfers between devices with their start and end apart: 63, of which 23 were waited for; matrix products, arithmetic and copies ran while one was open for 12% of the time, Pallas kernels for 22%

commit v1 on v0

--- a/solution.py
+++ b/solution.py
@@ -13,6 +13,7 @@
 ROPE_BASE = 10000.0
 LANES = 128
 KERNEL_HIGH = 2
+LOG2_E = 1.4426950408889634
 VMEM_BYTES = 44 * 1024 * 1024
 
 SHORT = pl.CostEstimate(flops=1000, bytes_accessed=1000, transcendentals=0)
@@ -525,6 +526,29 @@
     )(plane_place(), left, right)
 
 
+def gather_columns(matrices, gain_one, gain_two):
+    rows, width = matrices[0].shape
+    quarter = width // 4
+
+    def body(one_ref, two_ref, *refs):
+        out_ref = refs[-1]
+        pair = jnp.concatenate([one_ref[...], two_ref[...], jnp.zeros((6, rows), F32)], 0)
+        square = jnp.concatenate([pair, jnp.zeros((8, LANES - rows), F32)], 1)
+        square = jnp.concatenate([square, jnp.zeros((LANES - 8, LANES), F32)], 0)
+        gains = jnp.transpose(square)[:rows].astype(BF)
+        for i in range(4):
+            for at, ref in enumerate(refs[:-1]):
+                out_ref[i, :, at * quarter : (at + 1) * quarter] = ref[:, i * quarter : (i + 1) * quarter]
+            out_ref[i, :, len(matrices) * quarter :] = gains
+
+    return pl.pallas_call(
+        body,
+        out_shape=jax.ShapeDtypeStruct((4, rows, len(matrices) * quarter + LANES), BF),
+        cost_estimate=SHORT,
+        name="gather_columns",
+    )(gain_one.astype(F32)[None], gain_two.astype(F32)[None], *matrices)
+
+
 def group_place():
     unused, low, high, unused, core = place()
     return jnp.stack([2 * high + low, low, core]).astype(jnp.int32)
@@ -603,13 +627,26 @@
     ).astype(F32)
 
 
+def lane_sums(value):
+    total = value[:, :LANES]
+    for part in lane_blocks(value)[1:]:
+        total = total + part
+    return total
+
+
+def sums_as_row(value):
+    rows = value.shape[0]
+    padded = jnp.concatenate([value, jnp.zeros((LANES - rows, LANES), F32)], 0)
+    return jnp.sum(jnp.transpose(padded), axis=0, keepdims=True)[:, :rows]
+
+
 def join_columns(mine, recv, weights, gain, n_matrices):
     rows, cols = mine.shape[1:]
     size = cols // n_matrices
 
     def body(at_ref, mine_ref, recv_ref, gain_ref, *refs):
         weight_refs, out_refs = refs[: len(weights)], refs[len(weights) :]
-        total = jnp.zeros((rows, 1), F32)
+        total = jnp.zeros((rows, LANES), F32)
         for i in range(n_matrices):
             for z_low in range(2):
                 for core in range(2):
@@ -617,20 +654,19 @@
                     value = join_quarters(mine_ref, recv_ref, at_ref, i * size, size, z_low, core)
                     out_refs[i][:, at : at + size] = value
                     if i < len(weights):
-                        product = value * weight_refs[i][:, at : at + size].astype(F32)
-                        total = total + jnp.sum(product, axis=1, keepdims=True)
-        out_refs[-1][...] = total / gain_ref[...]
+                        total = total + lane_sums(value * weight_refs[i][:, at : at + size].astype(F32))
+        out_refs[-1][...] = sums_as_row(total) / gain_ref[...]
 
     vmem = pl.BlockSpec(memory_space=pltpu.VMEM)
     outs = pl.pallas_call(
         body,
         in_specs=[pl.BlockSpec(memory_space=pltpu.SMEM)] + [vmem] * (3 + len(weights)),
         out_specs=[vmem] * (n_matrices + 1),
-        out_shape=[jax.ShapeDtypeStruct((rows, 4 * size), F32)] * n_matrices + [jax.ShapeDtypeStruct((rows, 1), F32)],
+        out_shape=[jax.ShapeDtypeStruct((rows, 4 * size), F32)] * n_matrices + [jax.ShapeDtypeStruct((1, rows), F32)],
         cost_estimate=SHORT,
         name="join_columns",
-    )(group_place(), mine, recv, gain.astype(F32)[:, None], *weights)
-    return outs[:-1] + [outs[-1][:, 0]] if isinstance(outs, list) else list(outs[:-1]) + [outs[-1][:, 0]]
+    )(group_place(), mine, recv, gain.astype(F32)[None], *weights)
+    return list(outs[:-1]) + [outs[-1][0]]
 
 
 def join_units(mine, recv, weights, gain, n_blocks):
@@ -639,26 +675,26 @@
     size = 4 * quarter_size // n_blocks
 
     def body(at_ref, mine_ref, recv_ref, gain_ref, one_weight, two_weight, one_ref, two_ref, total_ref):
-        total = jnp.zeros((rows, 1), F32)
+        total = jnp.zeros((rows, LANES), F32)
         for half, (out_ref, weight_ref) in enumerate(((one_ref, one_weight), (two_ref, two_weight))):
             for block, (quarter, at) in enumerate(unit_blocks(n_blocks)):
                 start = half * quarter_size + at * size
                 out_ref[:, block * size : (block + 1) * size] = join_quarters(
                     mine_ref, recv_ref, at_ref, start, size, quarter // 2, quarter % 2
                 )
-            total = total + jnp.sum(out_ref[...] * weight_ref[...].astype(F32), axis=1, keepdims=True)
-        total_ref[...] = total / gain_ref[...]
+            total = total + lane_sums(out_ref[...] * weight_ref[...].astype(F32))
+        total_ref[...] = sums_as_row(total) / gain_ref[...]
 
     vmem = pl.BlockSpec(memory_space=pltpu.VMEM)
     one, two, total = pl.pallas_call(
         body,
         in_specs=[pl.BlockSpec(memory_space=pltpu.SMEM)] + [vmem] * 5,
         out_specs=[vmem] * 3,
-        out_shape=[jax.ShapeDtypeStruct((rows, 4 * quarter_size), F32)] * 2 + [jax.ShapeDtypeStruct((rows, 1), F32)],
+        out_shape=[jax.ShapeDtypeStruct((rows, 4 * quarter_size), F32)] * 2 + [jax.ShapeDtypeStruct((1, rows), F32)],
         cost_estimate=SHORT,
         name="join_units",
-    )(group_place(), mine, recv, gain.astype(F32)[:, None], *weights)
-    return one, two, total[:, 0]
+    )(group_place(), mine, recv, gain.astype(F32)[None], *weights)
+    return one, two, total[0]
 
 
 def pair_add(one, two):
@@ -787,6 +823,39 @@
     )(group_place(), mine, recv, x_one, gain, g_mine, g_recv, w_out)
 
 
+def input_back(mine, recv, x_all, gain, passed):
+    unused, seg_len, width = x_all.shape
+
+    def body(at_ref, mine_ref, recv_ref, x_ref, gain_ref, passed_ref, out_ref):
+        values = x_ref[0].astype(F32)
+        inverse = lax.rsqrt(jnp.mean(values * values, axis=-1, keepdims=True) + EPSILON)
+        normed = values * inverse
+        scaled = (mine_ref[...].astype(F32) + recv_ref[...].astype(F32)) * gain_ref[...]
+        mean = jnp.mean(scaled * normed, axis=-1, keepdims=True)
+        out_ref[...] = (passed_ref[...] + inverse * (scaled - normed * mean)).astype(BF)
+
+    tokens = pl.BlockSpec((seg_len, width), lambda i, at: (0, 0))
+    return pl.pallas_call(
+        body,
+        grid_spec=pltpu.PrefetchScalarGridSpec(
+            num_scalar_prefetch=1,
+            grid=(1,),
+            in_specs=[
+                tokens,
+                tokens,
+                pl.BlockSpec((1, seg_len, width), lambda i, at: (2 * at[1], 0, 0)),
+                pl.BlockSpec((1, width), lambda i, at: (0, 0)),
+                tokens,
+            ],
+            out_specs=tokens,
+        ),
+        out_shape=jax.ShapeDtypeStruct((seg_len, width), BF),
+        compiler_params=pltpu.CompilerParams(vmem_limit_bytes=VMEM_BYTES),
+        cost_estimate=SHORT,
+        name="input_back",
+    )(group_place(), mine, recv, x_all, gain, passed)
+
+
 def add_kernel(one, two):
     def body(one_ref, two_ref, out_ref):
         out_ref[...] = (one_ref[...].astype(F32) + two_ref[...].astype(F32)).astype(BF)
@@ -815,150 +884,178 @@
 N_GROUPS = 4
 
 
+def head_of(value, head):
+    return value[:, head * HD : (head + 1) * HD]
+
+
 def forward_kernel(q_ref, k_ref, v_ref, mine_ref, other_ref, *refs):
     key_refs, value_refs = refs[:N_GROUPS], refs[N_GROUPS : 2 * N_GROUPS]
     o_ref, of_ref, p_ref, pl_ref, inv_ref, s_ref, top_ref, total_ref, acc_ref = refs[2 * N_GROUPS :]
-    scale = HD ** (-0.5)
-    upper = pl.program_id(1) >= 2
+    heads = range(q_ref.shape[2] // HD)
+    scale = HD ** (-0.5) * LOG2_E
+    block = pl.program_id(0)
+    upper = block >= 2
     queries = q_ref[0]
     seg_len = queries.shape[0]
     per = key_refs[0].shape[1] // LANES
-    first = pl.program_id(1) % 2 == 0
+    first = block % 2 == 0
 
     def bias(at):
         return jnp.where(first, mine_ref[0, at], other_ref[0, at]).astype(F32)
 
-    local_bias = jnp.concatenate([bias(len(PIECES) * per + i) for i in range(cdiv(seg_len, LANES))], 1)
-    s_local = jnp.minimum(matmul_cols(queries, k_ref[0]) * scale, local_bias[:, :seg_len])
-
-    def score(t, top):
+    local_bias = jnp.concatenate([bias(len(PIECES) * per + i) for i in range(cdiv(seg_len, LANES))], 1)[:, :seg_len]
+    s_local = [
+        jnp.minimum(matmul_cols(head_of(queries, h), head_of(k_ref[0], h)) * scale, local_bias) for h in heads
+    ]
+
+    def score(t, tops):
         group, low = PIECES[t]
-        parts = lane_blocks(matmul_cols(queries, key_refs[group][low]) * scale)
+        keys = key_refs[group][low]
+        parts = [lane_blocks(matmul_cols(head_of(queries, h), head_of(keys, h)) * scale) for h in heads]
         for i in range(per):
-            part = jnp.minimum(parts[i], bias(t * per + i))
-            s_ref[t, :, i * LANES : (i + 1) * LANES] = part
-            top = part if top is None else jnp.maximum(top, part)
-        return top
-
-    top = None
+            limit = bias(t * per + i)
+            for h in heads:
+                part = jnp.minimum(parts[h][i], limit)
+                s_ref[h, t, :, i * LANES : (i + 1) * LANES] = part
+                tops[h] = part if tops[h] is None else jnp.maximum(tops[h], part)
+        return tops
+
+    tops = [None for h in heads]
     for t in range(N_COMMON):
-        top = score(t, top)
-    top_ref[...] = top
+        tops = score(t, tops)
+    for h in heads:
+        top_ref[h] = tops[h]
 
     @pl.when(upper)
     def more_scores():
-        more = top_ref[...]
+        tops = [top_ref[h] for h in heads]
         for t in range(N_COMMON, len(PIECES)):
-            more = score(t, more)
-        top_ref[...] = more
-
-    row_max = jnp.maximum(
-        jnp.max(s_local, axis=-1, keepdims=True), jnp.max(top_ref[...], axis=-1, keepdims=True)
-    )
-    e_local = jnp.exp(s_local - row_max)
-    low_local = e_local.astype(BF)
-    pl_ref[0, 0] = low_local
-
-    def weigh(t, total, acc):
+            tops = score(t, tops)
+        for h in heads:
+            top_ref[h] = tops[h]
+
+    row_max, e_local = [], []
+    for h in heads:
+        row_max.append(
+            jnp.maximum(
+                jnp.max(s_local[h], axis=-1, keepdims=True), jnp.max(top_ref[h], axis=-1, keepdims=True)
+            )
+        )
+        expo = jnp.exp2(s_local[h] - row_max[h])
+        e_local.append(jnp.sum(expo, axis=-1, keepdims=True))
+        chances = expo.astype(BF)
+        pl_ref[0, h] = chances
+        acc_ref[h] = matmul(chances, head_of(v_ref[0], h))
+
+    def weigh(t, h, total, acc):
         group, low = PIECES[t]
-        expo = jnp.exp(s_ref[t] - row_max)
+        expo = jnp.exp2(s_ref[h, t] - row_max[h])
         for part in lane_blocks(expo):
             total = part if total is None else total + part
         chances = expo.astype(BF)
-        p_ref[0, 0, t] = chances
-        return total, acc + matmul(chances, value_refs[group][low])
-
-    total, acc = None, matmul(low_local, v_ref[0])
-    for t in range(N_COMMON):
-        total, acc = weigh(t, total, acc)
-    total_ref[...] = total
-    acc_ref[...] = acc
+        p_ref[0, h, t] = chances
+        return total, acc + matmul(chances, head_of(value_refs[group][low], h))
+
+    for h in heads:
+        total, acc = None, acc_ref[h]
+        for t in range(N_COMMON):
+            total, acc = weigh(t, h, total, acc)
+        total_ref[h] = total
+        acc_ref[h] = acc
 
     @pl.when(upper)
     def more_values():
-        total, acc = total_ref[...], acc_ref[...]
-        for t in range(N_COMMON, len(PIECES)):
-            total, acc = weigh(t, total, acc)
-        total_ref[...] = total
-        acc_ref[...] = acc
-
-    row_total = jnp.sum(e_local, axis=-1, keepdims=True) + jnp.sum(total_ref[...], axis=-1, keepdims=True)
-    inverse = 1.0 / row_total
-    out = acc_ref[...] * inverse
-    of_ref[0] = out
-    o_ref[0] = out.astype(BF)
-    inv_ref[0, 0] = inverse
+        for h in heads:
+            total, acc = total_ref[h], acc_ref[h]
+            for t in range(N_COMMON, len(PIECES)):
+                total, acc = weigh(t, h, total, acc)
+            total_ref[h] = total
+            acc_ref[h] = acc
+
+    for h in heads:
+        inverse = 1.0 / (e_local[h] + jnp.sum(total_ref[h], axis=-1, keepdims=True))
+        out = acc_ref[h] * inverse
+        of_ref[0, :, h * HD : (h + 1) * HD] = out
+        o_ref[0, :, h * HD : (h + 1) * HD] = out.astype(BF)
+        inv_ref[0, h] = inverse
 
 
 def backward_local_kernel(do_ref, of_ref, q_ref, k_ref, v_ref, inv_ref, pl_ref, cos_ref, sin_ref, dkv_ref, dq_ref):
     scale = HD ** (-0.5)
-    d_out = do_ref[0]
-    delta = jnp.sum(d_out.astype(F32) * of_ref[0], axis=-1, keepdims=True)
-    chances = pl_ref[0, 0].astype(F32) * inv_ref[0, 0]
-    ds = (chances * (matmul_cols(d_out, v_ref[0]) - delta)).astype(BF)
-    dq_ref[0] = matmul(ds, k_ref[0])
-    dk = matmul_rows(ds, q_ref[0])
-    dkv_ref[0, 0] = ((dk * cos_ref[...] - pltpu.roll(dk, HD // 2, 1) * sin_ref[...]) * scale).astype(BF)
-    dkv_ref[1, 0] = matmul_rows(chances.astype(BF), d_out).astype(BF)
+    for h in range(q_ref.shape[2] // HD):
+        span = slice(h * HD, (h + 1) * HD)
+        d_out = do_ref[0, :, span]
+        delta = jnp.sum(d_out.astype(F32) * of_ref[0, :, span], axis=-1, keepdims=True)
+        chances = pl_ref[0, h].astype(F32) * inv_ref[0, h]
+        ds = (chances * (matmul_cols(d_out, v_ref[0, :, span]) - delta)).astype(BF)
+        dq_ref[0, :, span] = matmul(ds, k_ref[0, :, span])
+        dk = matmul_rows(ds, q_ref[0, :, span])
+        dkv_ref[0, 0, :, span] = (
+            (dk * cos_ref[...] - pltpu.roll(dk, HD // 2, 1) * sin_ref[...]) * scale
+        ).astype(BF)
+        dkv_ref[1, 0, :, span] = matmul_rows(chances.astype(BF), d_out).astype(BF)
 
 
 def backward_kernel(do_ref, of_ref, local_ref, inv_ref, p_ref, cos_ref, sin_ref, *refs):
     key_refs, value_refs = refs[:N_GROUPS], refs[N_GROUPS : 2 * N_GROUPS]
     out_ref, dq_ref = refs[2 * N_GROUPS :]
+    heads = range(do_ref.shape[2] // HD)
     scale = HD ** (-0.5)
-    upper = pl.program_id(1) >= 2
-    d_out = do_ref[0]
-    inverse = inv_ref[0, 0]
-    delta = jnp.sum(d_out.astype(F32) * of_ref[0], axis=-1, keepdims=True)
-
-    def piece(t, dq):
+    upper = pl.program_id(0) >= 2
+    d_out = [do_ref[0, :, h * HD : (h + 1) * HD] for h in heads]
+    inverse = [inv_ref[0, h] for h in heads]
+    delta = [
+        jnp.sum(d_out[h].astype(F32) * of_ref[0, :, h * HD : (h + 1) * HD], axis=-1, keepdims=True) for h in heads
+    ]
+
+    def piece(t, h, dq):
         group, low = PIECES[t]
-        dp = matmul_cols(d_out, value_refs[group][low])
-        ds = (p_ref[0, 0, t].astype(F32) * ((dp - delta) * inverse)).astype(BF)
-        return dq + matmul(ds, key_refs[group][low])
-
-    dq = local_ref[0]
-    for t in range(N_COMMON):
-        dq = piece(t, dq)
-    dq_ref[...] = dq
+        dp = matmul_cols(d_out[h], head_of(value_refs[group][low], h))
+        ds = (p_ref[0, h, t].astype(F32) * ((dp - delta[h]) * inverse[h])).astype(BF)
+        return dq + matmul(ds, head_of(key_refs[group][low], h))
+
+    for h in heads:
+        dq = local_ref[0, :, h * HD : (h + 1) * HD]
+        for t in range(N_COMMON):
+            dq = piece(t, h, dq)
+        dq_ref[h] = dq
 
     @pl.when(upper)
     def more():
-        dq = dq_ref[...]
-        for t in range(N_COMMON, len(PIECES)):
-            dq = piece(t, dq)
-        dq_ref[...] = dq
-
-    dq = dq_ref[...]
-    out_ref[0] = ((dq * cos_ref[...] - pltpu.roll(dq, HD // 2, 1) * sin_ref[...]) * scale).astype(BF)
-
-
-def attention_specs(piece_rows, seg_len):
-    head = pl.BlockSpec((1, seg_len, HD), lambda h, r: (r, 0, h))
-    piece = pl.BlockSpec((2, piece_rows, HD), lambda h, r: (0, 0, h))
-    p_spec = pl.BlockSpec((1, 1, len(PIECES), seg_len, piece_rows), lambda h, r: (r, h, 0, 0, 0))
-    pl_spec = pl.BlockSpec((1, 1, seg_len, seg_len), lambda h, r: (r, h, 0, 0))
-    inv_spec = pl.BlockSpec((1, 1, seg_len, 1), lambda h, r: (r, h, 0, 0))
-    return head, piece, p_spec, pl_spec, inv_spec
+        for h in heads:
+            dq = dq_ref[h]
+            for t in range(N_COMMON, len(PIECES)):
+                dq = piece(t, h, dq)
+            dq_ref[h] = dq
+
+    for h in heads:
+        dq = dq_ref[h]
+        out_ref[0, :, h * HD : (h + 1) * HD] = (
+            (dq * cos_ref[...] - pltpu.roll(dq, HD // 2, 1) * sin_ref[...]) * scale
+        ).astype(BF)
+
+
+def attention_specs(piece_rows, seg_len, width):
+    heads = width // HD
+    tokens = pl.BlockSpec((1, seg_len, width), lambda r: (r, 0, 0))
+    piece = pl.BlockSpec((2, piece_rows, width), lambda r: (0, 0, 0))
+    p_spec = pl.BlockSpec((1, heads, len(PIECES), seg_len, piece_rows), lambda r: (r, 0, 0, 0, 0))
+    pl_spec = pl.BlockSpec((1, heads, seg_len, seg_len), lambda r: (r, 0, 0, 0))
+    inv_spec = pl.BlockSpec((1, heads, seg_len, 1), lambda r: (r, 0, 0, 0))
+    return tokens, piece, p_spec, pl_spec, inv_spec
 
 
 def attention_forward(queries, keys, values, mask, other_mask, key_pieces, value_pieces):
     blocks, seg_len, width = queries.shape
     heads = width // HD
     piece_rows = key_pieces[0].shape[1]
-    head, piece, p_spec, pl_spec, inv_spec = attention_specs(piece_rows, seg_len)
+    tokens, piece, p_spec, pl_spec, inv_spec = attention_specs(piece_rows, seg_len, width)
+    mask_spec = pl.BlockSpec((1,) + mask.shape[1:], lambda r: (r // 2, 0, 0, 0))
     return pl.pallas_call(
         forward_kernel,
-        grid=(heads, blocks),
-        in_specs=[
-            head,
-            head,
-            head,
-            pl.BlockSpec((1,) + mask.shape[1:], lambda h, r: (r // 2, 0, 0, 0)),
-            pl.BlockSpec((1,) + mask.shape[1:], lambda h, r: (r // 2, 0, 0, 0)),
-        ]
-        + [piece] * (2 * N_GROUPS),
-        out_specs=[head, head, p_spec, pl_spec, inv_spec],
+        grid=(blocks,),
+        in_specs=[tokens, tokens, tokens, mask_spec, mask_spec] + [piece] * (2 * N_GROUPS),
+        out_specs=[tokens, tokens, p_spec, pl_spec, inv_spec],
         out_shape=[
             jax.ShapeDtypeStruct(queries.shape, BF),
             jax.ShapeDtypeStruct(queries.shape, F32),
@@ -967,10 +1064,10 @@
             jax.ShapeDtypeStruct((blocks, heads, seg_len, 1), F32),
         ],
         scratch_shapes=[
-            pltpu.VMEM((len(PIECES), seg_len, piece_rows), F32),
-            pltpu.VMEM((seg_len, LANES), F32),
-            pltpu.VMEM((seg_len, LANES), F32),
-            pltpu.VMEM((seg_len, HD), F32),
+            pltpu.VMEM((heads, len(PIECES), seg_len, piece_rows), F32),
+            pltpu.VMEM((heads, seg_len, LANES), F32),
+            pltpu.VMEM((heads, seg_len, LANES), F32),
+            pltpu.VMEM((heads, seg_len, HD), F32),
         ],
         compiler_params=pltpu.CompilerParams(vmem_limit_bytes=VMEM_BYTES),
         cost_estimate=SHORT,
@@ -980,13 +1077,13 @@
 
 def attention_backward_local(d_out, out_f32, queries, keys, values, inverse, p_local, cosine, sine):
     blocks, seg_len, width = queries.shape
-    head, unused, unused, pl_spec, inv_spec = attention_specs(seg_len, seg_len)
-    table = pl.BlockSpec((seg_len, HD), lambda h, r: (0, 0))
+    tokens, unused, unused, pl_spec, inv_spec = attention_specs(seg_len, seg_len, width)
+    table = pl.BlockSpec((seg_len, HD), lambda r: (0, 0))
     return pl.pallas_call(
         backward_local_kernel,
-        grid=(width // HD, blocks),
-        in_specs=[head, head, head, head, head, inv_spec, pl_spec, table, table],
-        out_specs=[pl.BlockSpec((2, 1, seg_len, HD), lambda h, r: (0, r, 0, h)), head],
+        grid=(blocks,),
+        in_specs=[tokens, tokens, tokens, tokens, tokens, inv_spec, pl_spec, table, table],
+        out_specs=[pl.BlockSpec((2, 1, seg_len, width), lambda r: (0, r, 0, 0)), tokens],
         out_shape=[
             jax.ShapeDtypeStruct((2, blocks, seg_len, width), BF),
             jax.ShapeDtypeStruct(queries.shape, F32),
@@ -999,17 +1096,16 @@
 
 def attention_backward(d_out, out_f32, dq_local, inverse, p_memory, cosine, sine, key_pieces, value_pieces):
     blocks, seg_len, width = d_out.shape
-    heads = width // HD
     piece_rows = key_pieces[0].shape[1]
-    head, piece, p_spec, unused, inv_spec = attention_specs(piece_rows, seg_len)
-    table = pl.BlockSpec((seg_len, HD), lambda h, r: (0, 0))
+    tokens, piece, p_spec, unused, inv_spec = attention_specs(piece_rows, seg_len, width)
+    table = pl.BlockSpec((seg_len, HD), lambda r: (0, 0))
     return pl.pallas_call(
         backward_kernel,
-        grid=(heads, blocks),
-        in_specs=[head, head, head, inv_spec, p_spec, table, table] + [piece] * (2 * N_GROUPS),
-        out_specs=head,
+        grid=(blocks,),
+        in_specs=[tokens, tokens, tokens, inv_spec, p_spec, table, table] + [piece] * (2 * N_GROUPS),
+        out_specs=tokens,
         out_shape=jax.ShapeDtypeStruct((blocks, seg_len, width), BF),
-        scratch_shapes=[pltpu.VMEM((seg_len, HD), F32)],
+        scratch_shapes=[pltpu.VMEM((width // HD, seg_len, HD), F32)],
         compiler_params=pltpu.CompilerParams(vmem_limit_bytes=VMEM_BYTES),
         cost_estimate=SHORT,
         name="attention_backward",
@@ -1125,11 +1221,14 @@
     def by_quarter(value):
         return [value[:, i * quarter : (i + 1) * quarter] for i in range(4)]
 
-    gains = jnp.concatenate(
+    gains = None if width // n_devices % 16 == 0 else jnp.concatenate(
         [gain_attn[:, None], gain_ffn[:, None], jnp.zeros((gain_attn.shape[0], LANES - 2), BF)], 1
     )
-    stacked = [by_quarter(w) for w in (w_query, w_key, w_value, w_out)]
-    qo = jnp.stack([jnp.concatenate([s[i] for s in stacked] + [gains], 1) for i in range(4)])
+    if gains is None:
+        qo = gather_columns((w_query, w_key, w_value, w_out), gain_attn, gain_ffn)
+    else:
+        stacked = [by_quarter(w) for w in (w_query, w_key, w_value, w_out)]
+        qo = jnp.stack([jnp.concatenate([s[i] for s in stacked] + [gains], 1) for i in range(4)])
 
     def core_quarters(value, side):
         return jnp.stack([cut(value, side * quarter, quarter), cut(value, (2 + side) * quarter, quarter)])
@@ -1239,8 +1338,9 @@
         out_low, out_f32, p_memory, p_local, inverse = attention_forward(
             queries, keys, values, mask, other_mask, key_pieces, value_pieces
         )
-        out_low, gate, upw, g_recv, u_recv, down_a, a_recv, down_b, wo_near, wo_far, g_own = fence(
-            out_low, gate, upw, g_recv, u_recv, down_a, a_recv, down_b, wo_near, wo_far, g_own
+        g_far = flip_z(g_own)
+        out_low, gate, upw, g_recv, u_recv, down_a, a_recv, down_b, wo_near, wo_far, g_own, g_far = fence(
+            out_low, gate, upw, g_recv, u_recv, down_a, a_recv, down_b, wo_near, wo_far, g_own, g_far
         )
     else:
         qo = gather_high(ordered(qo_keep[None], qo_near[None], low, 0)[None, :, None, None])
@@ -1267,6 +1367,7 @@
         wo_near = w_b[:, :quarter]
         out_low, out_f32, log_total = stream_forward(queries, keys, values, live_all, allow, memory)
         g_recv, u_recv, a_recv, wo_far = flip_x(gate), flip_y(upw), flip_x(down_a), flip_z(wo_near)
+        g_far = flip_z(g_own)
 
     h_one = h_one.reshape(group_tokens, width)
     inv_one = inv_one.reshape(group_tokens, 1)
@@ -1279,7 +1380,6 @@
     g_recv, u_recv = flip_y(gate), flip_x(upw)
     wo_both = jnp.stack([wo_near, wo_far])
     wo_recv = flip_core(wo_both)
-    g_far = flip_z(g_own)
     wo = join_four(wo_both, wo_recv, False)
     att_near, att_far, gate, upw, g_recv, u_recv, down_b, wo, g_own, g_far = fence(
         att_near, att_far, gate, upw, g_recv, u_recv, down_b, wo, g_own, g_far
@@ -1308,12 +1408,14 @@
     d_gate = (d_hidden * up_out * sigma * (1.0 + gate_out * (1.0 - sigma))).astype(BF)
     d_up = (d_hidden * swish).astype(BF)
     sums_keep, sums_give = back_project([d_gate, d_up], [wg, wu])
-    sums = add_low(sums_keep, flip_core(sums_give))
-    sums, hidden, h_two, d_gate, d_up, wd = fence(sums, hidden, h_two, d_gate, d_up, wd)
-
+    sums_recv = flip_core(sums_give)
+    (keep_g, give_g), (keep_u, give_u) = gradient((h_two, [d_gate], "x", None), (h_two, [d_up], "y", None))
+    sums_keep, sums_recv, keep_g, give_g, keep_u, give_u, hidden, wd = fence(
+        sums_keep, sums_recv, keep_g, give_g, keep_u, give_u, hidden, wd
+    )
+
+    sums = add_kernel(sums_keep, sums_recv)
     far_sums = flip_z(sums)
-    (keep_g, give_g), (keep_u, give_u) = gradient((h_two, [d_gate], "x", None), (h_two, [d_up], "y", None))
-    keep_g, give_g, keep_u, give_u, hidden, wd = fence(keep_g, give_g, keep_u, give_u, hidden, wd)
     recv_g, recv_u = flip_x(give_g), flip_y(give_u)
     down_keep, down_give = back_project([hidden], [wd], False)
     down_recv = flip_core(down_give)
@@ -1384,16 +1486,16 @@
         keep_q, recv_q, keep_kvo, recv_kvo, keep_wd, recv_wd, d_h_keep, d_h_give, gu_keep, gu_give = fence(
             keep_q, recv_q, keep_kvo, recv_kvo, keep_wd, recv_wd, d_h_keep, d_h_give, gu_keep, gu_give
         )
+        *parts, wd_own = plane_sort((keep_q,) + tuple(recv_q), (keep_kvo, recv_kvo), units=(keep_wd, recv_wd))
+        parts, d_h_give, wd_own = fence(parts, d_h_give, wd_own)
         d_h_recv = flip_core(d_h_give)
-        *parts, wd_own = plane_sort((keep_q,) + tuple(recv_q), (keep_kvo, recv_kvo), units=(keep_wd, recv_wd))
         flips = z_flips(parts)
         d_h_own, d_h_give = pair_add(d_h_keep, d_h_recv)
         d_h_recv = flip_z(d_h_give)
         gu_recv = flip_core(gu_give)
         sum_wg, sum_wu, grad_g_ffn = join_units(gu_keep, gu_recv, (w_gate, w_up), gain_ffn, n_devices)
-        kept, flips, d_h_own, d_h_recv, wd_own, sum_wg, sum_wu = fence(
-            parts[0], flips, d_h_own, d_h_recv, wd_own, sum_wg, sum_wu
-        )
+        grad_x = input_back(d_h_own, d_h_recv, x_all, g_attn[None], d_x_own)
+        kept, flips, grad_x, wd_own, sum_wg, sum_wu = fence(parts[0], flips, grad_x, wd_own, sum_wg, sum_wu)
         qkvo_keep, qkvo_give = z_merge(kept, *flips)
         qkvo_recv = flip_core(qkvo_give)
         wd_recv = flips[1][kept.shape[0] : kept.shape[0] + wd_own.shape[0]]
@@ -1422,16 +1524,13 @@
         d_h_keep, d_h_give = back_project([d_q, d_kv[0], d_kv[1]], w_thirds)
         d_h_own, d_h_give = pair_add(d_h_keep, flip_core(d_h_give))
         d_h_recv = flip_z(d_h_give)
+        grad_x = input_back(d_h_own, d_h_recv, x_all, g_attn[None], d_x_own)
         sum_wd = reduce_high(add_low(keep_wd, recv_wd)[:, None])[0].astype(F32)
         sum_wg, sum_wu, grad_g_ffn = join_units(gu_keep, gu_recv, (w_gate, w_up), gain_ffn, n_devices)
     layer_output = (cut(x_one, own, seg_len, 0) + down_own.astype(F32) + down_recv.astype(F32)).astype(BF)
     sum_q, sum_k, sum_v, sum_o, grad_g_attn = join_columns(
         qkvo_keep, qkvo_recv, (w_query, w_key, w_value), gain_attn, 4
     )
-    d_h_one = d_h_own.astype(F32) + d_h_recv.astype(F32)
-    x_own = cut(x_float, own, seg_len, 0)
-    d_x_first, unused = norm_backward(x_own, cut(inv_one, own, seg_len, 0), g_attn, d_h_one)
-    grad_x = (d_x_own + d_x_first).astype(BF)
     return (
         layer_output[None],
         grad_x[None],

time: 319 us -> 313 us (0.981)
  waiting for transfers between devices: 91.8 us -> 97.7 us
  Pallas kernels: 89.1 us -> 84.8 us
  other arithmetic: 27.4 us -> 24 us
    ppermute x60, waiting for transfers between devices: 89.5 us -> 95.9 us  [flip(): return lax.ppermute(value, axis, [(i, i ^ bit) for i in range(count)])]
    pallas_call x3 -> x5, Pallas kernels: 32.9 us -> 27.7 us  [the longest x1 11 us: attention_forward(): pl.pallas_call(forward_kernel, grid=(blocks,), in_specs=[tokens, tokens,...]
    unnamed x209 -> x203, local copies, waits for them, and re-layouts: 13.4 us -> 18 us
  transfers between devices with their start and end apart: 63 -> 63, of which waited for: 23 -> 30; matrix products, arithmetic and copies ran while one was open for 12% -> 10% of each run, Pallas kernels for 22% -> 22%
where the time goes in v1:
time: 313 us; the launch traced here: 312 us
  waiting for transfers between devices  97.7 us (31%)
  Pallas kernels  84.8 us (27%)
  starting transfers between devices  69.9 us (22%)
  local copies, waits for them, and re-layouts  25.2 us (8%)
  other arithmetic  24 us (8%)
  matrix products  7.73 us (2%)
    ppermute x60, waiting for transfers between devices, flip(): return lax.ppermute(value, axis, [(i, i ^ bit) for i in range(count)])  95.9 us
    ppermute x60, starting transfers between devices, flip(): return lax.ppermute(value, axis, [(i, i ^ bit) for i in range(count)])  60.8 us
    unnamed x203, local copies, waits for them, and re-layouts  18 us
    pallas_call x1, Pallas kernels, attention_forward(): pl.pallas_call(forward_kernel, grid=(blocks,), in_specs=[tokens, tokens,...  11 us
    pallas_call x1, Pallas kernels, build_mask(): pl.pallas_call(lambda *refs: mask_kernel(n_cols, *refs), grid=(rows, quer...  10.6 us
    pallas_call x1, Pallas kernels, attention_backward(): pl.pallas_call(backward_kernel, grid=(blocks,), in_specs=[tokens, tokens,...  9.94 us
    pallas_call x3, Pallas kernels, gradient(): pl.pallas_call(body, grid_spec=pltpu.PrefetchScalarGridSpec(num_scalar_pr...  9.9 us
    ppermute x2, starting transfers between devices, cross(): return lax.ppermute(value, 'seg', up_high)  6.91 us
  transfers between devices with their start and end apart: 63, of which 30 were waited for; matrix products, arithmetic and copies ran while one was open for 10% of the time, Pallas kernels for 22%

profile of v1, /device:TPU:0, one launch (start us, length us, event | category | flops | bytes accessed | tf_op | source)
XLA Modules:
  0.0 311.8 jit_solution(2409048306614052529)
XLA Ops:
  2.3 3.1 collective-permute-start.2
  16.0 3.5 %collective-permute-start.4 = (bf16[64,1152]{1,0:T(8,128)(2,1)S(1)}, bf16[64,1152]{1,0:T(8,128)(2,1)}, u32[]{:S(2)}, u32[]{:S(2)}) collective-permute-start(bf16[64,1152]{1,0:T(8,128)(2,1)S(1)} %get-tuple-element.248), channel_id=1, source_target_pairs={{0,16},{4,20},{8,24},{12,28},{16,0},{20,4},{24,8},{28,12},{1,17},{... | collective-permute-start | bytes 442376 | tf_op jit(solution)/shard_map/ppermute | solution.py:31
  23.8 3.7 %collective-permute-done.3 = bf16[64,1152]{1,0:T(8,128)(2,1)S(1)} collective-permute-done((bf16[64,1152]{1,0:T(8,128)(2,1)}, bf16[64,1152]{1,0:T(8,128)(2,1)S(1)}, u32[]{:S(2)}, u32[]{:S(2)}) %collective-permute-start.3) | collective-permute-done | bytes 147488 | tf_op jit(solution)/shard_map/ppermute | solution.py:31
  27.5 3.5 %collective-permute-done.4 = bf16[64,1152]{1,0:T(8,128)(2,1)} collective-permute-done((bf16[64,1152]{1,0:T(8,128)(2,1)S(1)}, bf16[64,1152]{1,0:T(8,128)(2,1)}, u32[]{:S(2)}, u32[]{:S(2)}) %collective-permute-start.4) | collective-permute-done | bytes 147488 | tf_op jit(solution)/shard_map/ppermute | solution.py:31
  31.0 5.2 %collective-permute-done.6 = bf16[2,384,256]{2,1,0:T(8,128)(2,1)S(1)} collective-permute-done((bf16[2,384,256]{2,1,0:T(8,128)(2,1)S(1)}, bf16[2,384,256]{2,1,0:T(8,128)(2,1)S(1)}, u32[]{:S(2)}, u32[]{:S(2)}) %collective-permute-start.6) | collective-permute-done | bytes 393248 | tf_op jit(solution)/shard_map/ppermute | solution.py:31
  40.8 4.4 %collective-permute-start.10 = (bf16[2,384,256]{2,1,0:T(8,128)(2,1)S(1)}, bf16[2,384,256]{2,1,0:T(8,128)(2,1)S(1)}, u32[]{:S(2)}, u32[]{:S(2)}) collective-permute-start(bf16[2,384,256]{2,1,0:T(8,128)(2,1)S(1)} %get-tuple-element.505.refs_3_), channel_id=1, source_target_pairs={{0,16},{4,20},{8,24},{12,28},{1,17},{5,21},{9,25},{13,29},{2,18},{... | collective-permute-start | bytes 1179656 | tf_op jit(solution)/shard_map/ppermute | solution.py:1295
  47.8 10.6 %mask_build.1.mine_ref = bf16[2,23,192,128]{3,2,1,0:T(8,128)(2,1)S(1)} custom-call(s32[2,192,128]{2,1,0:T(8,128)S(1)} %copy.57.refs_0_, s32[2,1,256]{2,1,0:T(1,128)S(1)} %pad.4.refs_1_), custom_call_target="tpu_custom_call" | custom-call | flops 12000000000 | bytes 3000000 | tf_op jit(solution)/shard_map/mask_build/pallas_call | solution.py:314
  59.3 3.1 collective-permute-done.12
  74.3 6.3 %collective-permute-done.15 = bf16[2,2,1,2,64,384]{5,4,3,2,1,0:T(8,128)(2,1)S(1)} collective-permute-done((bf16[2,2,1,2,64,384]{5,4,3,2,1,0:T(8,128)(2,1)S(1)}, bf16[2,2,1,2,64,384]{5,4,3,2,1,0:T(8,128)(2,1)S(1)}, u32[]{:S(2)}, u32[]{:S(2)}) %collective-permute-start.15) | collective-permute-done | bytes 393248 | tf_op jit(solution)/shard_map/ppermute | solution.py:31
  81.5 6.5 %collective-permute-done.17.refs_1_ = bf16[2,384,256]{2,1,0:T(8,128)(2,1)S(1)} collective-permute-done((bf16[2,384,256]{2,1,0:T(8,128)(2,1)S(1)}, bf16[2,384,256]{2,1,0:T(8,128)(2,1)S(1)}, u32[]{:S(2)}, u32[]{:S(2)}) %collective-permute-start.17) | collective-permute-done | bytes 393248 | tf_op jit(solution)/shard_map/ppermute | solution.py:31
  94.8 3.2 %project.1 = (bf16[4,192,256]{2,1,0:T(8,128)(2,1)S(1)}, bf16[4,192,256]{2,1,0:T(8,128)(2,1)S(1)}, bf16[4,192,256]{2,1,0:T(8,128)(2,1)S(1)}, bf16[4,192,1024]{2,1,0:T(8,128)(2,1)S(1)}, f32[4,192,1]{2,1,0:T(8,128)}) custom-call(bf16[4,192,1024]{2,1,0:T(8,128)(2,1)S(1)} %bitcast.144, bf16[1024,768]{1,0:T(8,128)(2,1)S(1)} %bitcast.146, ...), custom_call_target="tpu_custom_call" | custom-call | flops 1000 | bytes 1000 | tf_op jit(solution)/shard_map/project/pallas_call | solution.py:361
  99.7 10.4 %collective-permute-done.22 = bf16[2,1,2,64,704]{4,3,2,1,0:T(8,128)(2,1)S(1)} collective-permute-done((bf16[2,1,2,64,704]{4,3,2,1,0:T(8,128)(2,1)S(1)}, bf16[2,1,2,64,704]{4,3,2,1,0:T(8,128)(2,1)S(1)}, u32[]{:S(2)}, u32[]{:S(2)}) %collective-permute-start.22) | collective-permute-done | bytes 360480 | tf_op jit(solution)/shard_map/ppermute | solution.py:31
  118.0 11.0 %attention_forward.1 = (bf16[4,192,256]{2,1,0:T(8,128)(2,1)S(1)}, f32[4,192,256]{2,1,0:T(8,128)S(1)}, bf16[4,2,7,192,384]{4,3,2,1,0:T(8,128)(2,1)}, bf16[4,2,192...) custom-call(bf16[4,192,256]{2,1,0:T(8,128)(2,1)S(1)} %get-tuple-element.289.q_ref, ...), custom_call_target="tpu_custom_call" | custom-call | flops 1000 | bytes 1000 | tf_op jit(solution)/shard_map/attention_forward/pallas_call | solution.py:1054
  152.0 5.6 %collective-permute-done.31 = bf16[2,2,2,1,64,704]{5,4,1,0,3,2:T(8,128)(2,1)} collective-permute-done((bf16[2,2,2,1,64,704]{5,4,1,0,3,2:T(8,128)(2,1)}, bf16[2,2,2,1,64,704]{5,4,1,0,3,2:T(8,128)(2,1)}, u32[]{:S(2)}, u32[]{:S(2)}) %collective-permute-start.31) | collective-permute-done | bytes 720928 | tf_op jit(solution)/shard_map/ppermute | solution.py:31
  175.6 3.5 %back_project.3 = (bf16[2,192,1024]{2,1,0:T(8,128)(2,1)S(1)}, bf16[2,192,1024]{2,1,0:T(8,128)(2,1)}) custom-call(bf16[768,704]{1,0:T(8,128)(2,1)S(1)} %get-tuple-element.472.refs_0_.refs_1_, bf16[768,704]{1,0:T(8,128)(2,1)S(1)} %get-tuple-element.471.refs_1_.refs_2_, bf16[1024,704]{1,0:T(8,128)(2,1)S(1)} %bitcast.154, bf16[1024,704]{1,0:T(8,128)(2,1)S(1)} %bitcast.156), custom_call_target="tpu_custom_call" | custom-call | flops 1000 | bytes 1000 | tf_op jit(solution)/shard_map/back_project/pallas_call | solution.py:733
  184.5 4.3 %gradient.3 = (bf16[8,64,704]{2,1,0:T(8,128)(2,1)S(1)}, bf16[8,64,704]{2,1,0:T(8,128)(2,1)S(1)}, bf16[8,64,704]{2,1,0:T(8,128)(2,1)S(1)}, bf16[8,64,704]{2,1,0:T(8,128)(2,1)S(1)}) custom-call(s32[3]{0:T(128)S(1)} %pad_add_fusion.2.at_ref, bf16[768,1024]{1,0:T(8,128)(2,1)S(1)} %copy-done.10, bf16[768,704]{1,0:T(8,128)(2,1)S(1)} %copy-done.15, ...), custom_call_target="tpu_custom_call" | custom-call | flops 1000 | bytes 1000 | tf_op jit(solution)/shard_map/gradient/pallas_call | solution.py:449
  201.6 13.0 %collective-permute-done.39.recv_ref = bf16[8,64,704]{2,1,0:T(8,128)(2,1)S(1)} collective-permute-done((bf16[8,64,704]{2,1,0:T(8,128)(2,1)S(1)}, bf16[8,64,704]{2,1,0:T(8,128)(2,1)S(1)}, u32[]{:S(2)}, u32[]{:S(2)}) %collective-permute-start.39) | collective-permute-done | bytes 720928 | tf_op jit(solution)/shard_map/ppermute | solution.py:31
  219.2 4.8 %branch_back.1 = (bf16[4,192,1024]{2,1,0:T(8,128)(2,1)S(1)}, bf16[4,192,256]{2,1,0:T(8,128)(2,1)S(1)}, f32[192,1024]{1,0:T(8,128)S(1)}) custom-call(s32[3]{0:T(128)S(1)} %pad_add_fusion.1.at_ref, bf16[2,192,1024]{2,1,0:T(8,128)(2,1)S(1)} %add_kernel.3.mine_ref, bf16[2,192,1024]{2,1,0:T(8,128)(2,1)S(1)} %collective-permute-done.42.recv_ref, ...), custom_call_target="tpu_custom_call" | custom-call | flops 1000 | bytes 1000 | tf_op jit(solution)/shard_map/branch_back/pallas_call | solution.py:795
  229.6 3.3 %attention_backward_local.1 = (bf16[2,4,192,256]{3,2,1,0:T(8,128)(2,1)S(1)}, f32[4,192,256]{2,1,0:T(8,128)S(1)}) custom-call(bf16[4,192,256]{2,1,0:T(8,128)(2,1)S(1)} %get-tuple-element.357.do_ref, f32[4,192,256]{2,1,0:T(8,128)S(1)} %copy-done.20, bf16[4,192,256]{2,1,0:T(8,128)(2,1)S(1)} %copy-done.46, bf16[4,192,256]{2,1,0:T(8,128)(2,1)S(1)} %copy-done.48, ...), custom_call_target="tpu_custom_call" | custom-call | flops 1000 | bytes 1000 | tf_op jit(solution)/shard_map/attention_backward_local/pallas_call | solution.py:1082
  234.3 3.2 %gradient.4 = (bf16[8,64,512]{2,1,0:T(8,128)(2,1)S(1)}, bf16[8,64,512]{2,1,0:T(8,128)(2,1)S(1)}, bf16[8,64,256]{2,1,0:T(8,128)(2,1)S(1)}, bf16[8,64,256]{2,1,0:T(8,128)(2,1)S(1)}) custom-call(s32[3]{0:T(128)S(1)} %pad_add_fusion.2.at_ref, bf16[768,1024]{1,0:T(8,128)(2,1)S(1)} %bitcast.157, bf16[768,1024]{1,0:T(8,128)(2,1)S(1)} %copy-done.8, ...), custom_call_target="tpu_custom_call" | custom-call | flops 1000 | bytes 1000 | tf_op jit(solution)/shard_map/gradient/pallas_call | solution.py:449
  243.0 3.4 %collective-permute-start.50 = (bf16[64,1408]{1,0:T(8,128)(2,1)S(1)}, bf16[64,1408]{1,0:T(8,128)(2,1)S(1)}, u32[]{:S(2)}, u32[]{:S(2)}) collective-permute-start(bf16[64,1408]{1,0:T(8,128)(2,1)S(1)} %get-tuple-element.403), channel_id=1, source_target_pairs={{0,24},{4,28},{8,16},{12,20},{16,8},{20,12},{24,0},{28,4},{1,25},{... | collective-permute-start | bytes 540680 | tf_op jit(solution)/shard_map/ppermute | solution.py:31
  246.5 9.9 %attention_backward.1 = bf16[4,192,256]{2,1,0:T(8,128)(2,1)S(1)} custom-call(bf16[4,192,256]{2,1,0:T(8,128)(2,1)S(1)} %get-tuple-element.357.do_ref, f32[4,192,256]{2,1,0:T(8,128)S(1)} %copy-done.20, f32[4,192,256]{2,1,0:T(8,128)S(1)} %get-tuple-element.384.local_ref, f32[4,2,192,1]{3,2,1,0:T(8,128)S(1)} %copy-done.22, ...), custom_call_target="tpu_custom_call" | custom-call | flops 1000 | bytes 1000 | tf_op jit(solution)/shard_map/attention_backward/pallas_call | solution.py:1102
  292.1 7.8 %collective-permute-done.60.recv_ref = bf16[192,1024]{1,0:T(8,128)(2,1)S(1)} collective-permute-done((bf16[192,1024]{1,0:T(8,128)(2,1)}, bf16[192,1024]{1,0:T(8,128)(2,1)S(1)}, u32[]{:S(2)}, u32[]{:S(2)}) %collective-permute-start.60) | collective-permute-done | bytes 393248 | tf_op jit(solution)/shard_map/ppermute | solution.py:31
  302.8 4.0 %collective-permute-done.58.three_ref = bf16[64,1024]{1,0:T(8,128)(2,1)} collective-permute-done((bf16[64,1024]{1,0:T(8,128)(2,1)}, bf16[64,1024]{1,0:T(8,128)(2,1)}, u32[]{:S(2)}, u32[]{:S(2)}) %collective-permute-start.58) | collective-permute-done | bytes 131104 | tf_op jit(solution)/shard_map/ppermute | solution.py:31
  (429 shorter events, 172.0 us)
Async XLA Ops:
  5.4 17.2 %collective-permute-start.7 = (bf16[1,1,1,1,88,1024]{5,4,3,2,1,0:T(8,128)(2,1)}, bf16[1,1,1,1,88,1024]{5,4,3,2,1,0:T(8,128)(2,1)S(1)}, u32[]{:S(2)}, u32[]{:S(2)}) collective-permute-start(bf16[1,1,1,1,88,1024]{5,4,3,2,1,0:T(8,128)(2,1)} %bitcast.190), channel_id=1, source_target_pairs={{0,16},{4,20},{8,24},{12,28},{16,0},{20,4},{24,8},{28,12},{1,17},{... | collective-permute-start | bytes 540680 | tf_op jit(solution)/shard_map/ppermute | solution.py:31
  39.3 23.1 %collective-permute-start.11 = (bf16[2,384,256]{2,1,0:T(8,128)(2,1)S(1)}, bf16[2,384,256]{2,1,0:T(8,128)(2,1)S(1)}, u32[]{:S(2)}, u32[]{:S(2)}) collective-permute-start(bf16[2,384,256]{2,1,0:T(8,128)(2,1)S(1)} %get-tuple-element.505.refs_3_), channel_id=1, source_target_pairs={{0,4},{4,0},{8,12},{12,8},{16,20},{20,16},{24,28},{28,24},{1,5},{5... | collective-permute-start | bytes 1179656 | tf_op jit(solution)/shard_map/ppermute | solution.py:31
  40.8 21.6 %collective-permute-start.10 = (bf16[2,384,256]{2,1,0:T(8,128)(2,1)S(1)}, bf16[2,384,256]{2,1,0:T(8,128)(2,1)S(1)}, u32[]{:S(2)}, u32[]{:S(2)}) collective-permute-start(bf16[2,384,256]{2,1,0:T(8,128)(2,1)S(1)} %get-tuple-element.505.refs_3_), channel_id=1, source_target_pairs={{0,16},{4,20},{8,24},{12,28},{1,17},{5,21},{9,25},{13,29},{2,18},{... | collective-permute-start | bytes 1179656 | tf_op jit(solution)/shard_map/ppermute | solution.py:1295
  63.2 24.9 %collective-permute-start.19 = (bf16[2,192,1024]{2,1,0:T(8,128)(2,1)S(1)}, bf16[2,192,1024]{2,1,0:T(8,128)(2,1)S(1)}, u32[]{:S(2)}, u32[]{:S(2)}) collective-permute-start(bf16[2,192,1024]{2,1,0:T(8,128)(2,1)S(1)} %pad_maximum_fusion.8), channel_id=1, source_target_pairs={{0,1},{1,0},{2,3},{3,2},{4,5},{5,4},{6,7},{7,6},{8,9},{9,8},{10,11... | collective-permute-start | bytes 2359304 | tf_op jit(solution)/shard_map/ppermute | solution.py:31
  63.3 24.7 %collective-permute-start.14 = (bf16[2,2,2,1,64,768]{5,4,3,2,1,0:T(8,128)(2,1)S(1)}, bf16[2,2,2,1,64,768]{5,4,3,2,1,0:T(8,128)(2,1)S(1)}, u32[]{:S(2)}, u32[]{:S(2)}) collective-permute-start(bf16[2,2,2,1,64,768]{5,4,3,2,1,0:T(8,128)(2,1)S(1)} %pad_maximum_fusion.7), channel_id=1, source_target_pairs={{0,2},{1,3},{2,0},{3,1},{4,6},{5,7},{6,4},{7,5},{8,10},{9,11},{10,... | collective-permute-start | bytes 2359304 | tf_op jit(solution)/shard_map/ppermute | solution.py:31
  88.1 22.1 %collective-permute-start.24 = (bf16[2,23,192,128]{3,2,1,0:T(8,128)(2,1)S(1)}, bf16[2,23,192,128]{3,2,1,0:T(8,128)(2,1)S(1)}, u32[]{:S(2)}, u32[]{:S(2)}) collective-permute-start(bf16[2,23,192,128]{3,2,1,0:T(8,128)(2,1)S(1)} %mask_build.1.mine_ref), channel_id=1, source_target_pairs={{0,1},{1,0},{2,3},{3,2},{4,5},{5,4},{6,7},{7,6},{8,9},{9,8},{10,11... | collective-permute-start | bytes 6782984 | tf_op jit(solution)/shard_map/ppermute | solution.py:31
  89.5 20.6 %collective-permute-start.22 = (bf16[2,1,2,64,704]{4,3,2,1,0:T(8,128)(2,1)S(1)}, bf16[2,1,2,64,704]{4,3,2,1,0:T(8,128)(2,1)S(1)}, u32[]{:S(2)}, u32[]{:S(2)}) collective-permute-start(bf16[2,1,2,64,704]{4,3,2,1,0:T(8,128)(2,1)S(1)} %maximum_bitcast_fusion.1), channel_id=1, source_target_pairs={{0,16},{4,20},{8,24},{12,28},{16,0},{20,4},{24,8},{28,12},{1,17},{... | collective-permute-start | bytes 1081352 | tf_op jit(solution)/shard_map/ppermute | solution.py:31
  90.2 20.0 %collective-permute-start.20 = (bf16[2,384,256]{2,1,0:T(8,128)(2,1)S(1)}, bf16[2,384,256]{2,1,0:T(8,128)(2,1)S(1)}, u32[]{:S(2)}, u32[]{:S(2)}) collective-permute-start(bf16[2,384,256]{2,1,0:T(8,128)(2,1)S(1)} %collective-permute-done.16.refs_4_), channel_id=1, source_target_pairs={{0,4},{4,0},{8,12},{12,8},{16,20},{20,16},{24,28},{28,24},{1,5},{5... | collective-permute-start | bytes 1179656 | tf_op jit(solution)/shard_map/ppermute | solution.py:31
  90.7 19.4 %collective-permute-start.21 = (bf16[2,384,256]{2,1,0:T(8,128)(2,1)S(1)}, bf16[2,384,256]{2,1,0:T(8,128)(2,1)S(1)}, u32[]{:S(2)}, u32[]{:S(2)}) collective-permute-start(bf16[2,384,256]{2,1,0:T(8,128)(2,1)S(1)} %get-tuple-element.283.refs_7_), channel_id=1, source_target_pairs={{0,4},{4,0},{8,12},{12,8},{16,20},{20,16},{24,28},{28,24},{1,5},{5... | collective-permute-start | bytes 1179656 | tf_op jit(solution)/shard_map/ppermute | solution.py:31
  110.2 21.4 %collective-permute-start.29 = (bf16[192,1024]{1,0:T(8,128)(2,1)S(1)}, bf16[192,1024]{1,0:T(8,128)(2,1)S(1)}, u32[]{:S(2)}, u32[]{:S(2)}) collective-permute-start(bf16[192,1024]{1,0:T(8,128)(2,1)S(1)} %bitcast.187), channel_id=1, source_target_pairs={{0,8},{4,12},{8,0},{12,4},{16,24},{20,28},{24,16},{28,20},{1,9},{5... | collective-permute-start | bytes 1179656 | tf_op jit(solution)/shard_map/ppermute | solution.py:31
  113.0 19.6 %collective-permute-start.28 = (bf16[1024,256]{1,0:T(8,128)(2,1)S(1)}, bf16[1024,256]{1,0:T(8,128)(2,1)S(1)}, u32[]{:S(2)}, u32[]{:S(2)}) collective-permute-start(bf16[1024,256]{1,0:T(8,128)(2,1)S(1)} %slice.90), channel_id=1, source_target_pairs={{0,8},{4,12},{8,0},{12,4},{16,24},{20,28},{24,16},{28,20},{1,9},{5... | collective-permute-start | bytes 1572872 | tf_op jit(solution)/shard_map/ppermute | solution.py:31
  133.7 18.3 %collective-permute-start.32 = (bf16[2,2,1,2,64,704]{5,4,3,2,1,0:T(8,128)(2,1)}, bf16[2,2,1,2,64,704]{5,4,3,2,1,0:T(8,128)(2,1)}, u32[]{:S(2)}, u32[]{:S(2)}) collective-permute-start(bf16[2,2,1,2,64,704]{5,4,3,2,1,0:T(8,128)(2,1)} %pad_maximum_fusion.11), channel_id=1, source_target_pairs={{0,4},{4,0},{8,12},{12,8},{16,20},{20,16},{24,28},{28,24},{1,5},{5... | collective-permute-start | bytes 2162696 | tf_op jit(solution)/shard_map/ppermute | solution.py:31
  137.3 20.3 %collective-permute-start.31 = (bf16[2,2,2,1,64,704]{5,4,1,0,3,2:T(8,128)(2,1)}, bf16[2,2,2,1,64,704]{5,4,1,0,3,2:T(8,128)(2,1)}, u32[]{:S(2)}, u32[]{:S(2)}) collective-permute-start(bf16[2,2,2,1,64,704]{5,4,1,0,3,2:T(8,128)(2,1)} %pad_maximum_fusion.10), channel_id=1, source_target_pairs={{0,2},{1,3},{2,0},{3,1},{4,6},{5,7},{6,4},{7,5},{8,10},{9,11},{10,... | collective-permute-start | bytes 2162696 | tf_op jit(solution)/shard_map/ppermute | solution.py:31
  191.4 25.3 %collective-permute-start.38 = (bf16[2,192,1024]{2,1,0:T(8,128)(2,1)S(1)}, bf16[2,192,1024]{2,1,0:T(8,128)(2,1)S(1)}, u32[]{:S(2)}, u32[]{:S(2)}) collective-permute-start(bf16[2,192,1024]{2,1,0:T(8,128)(2,1)S(1)} %add_kernel.2.one_ref), channel_id=1, source_target_pairs={{0,8},{4,12},{8,0},{12,4},{16,24},{20,28},{24,16},{28,20},{1,9},{5... | collective-permute-start | bytes 2359304 | tf_op jit(solution)/shard_map/ppermute | solution.py:31
  194.5 22.1 %collective-permute-start.41 = (bf16[2,192,1024]{2,1,0:T(8,128)(2,1)S(1)}, bf16[2,192,1024]{2,1,0:T(8,128)(2,1)S(1)}, u32[]{:S(2)}, u32[]{:S(2)}) collective-permute-start(bf16[2,192,1024]{2,1,0:T(8,128)(2,1)S(1)} %get-tuple-element.344), channel_id=1, source_target_pairs={{0,1},{1,0},{2,3},{3,2},{4,5},{5,4},{6,7},{7,6},{8,9},{9,8},{10,11... | collective-permute-start | bytes 2359304 | tf_op jit(solution)/shard_map/ppermute | solution.py:31
  194.6 20.0 %collective-permute-start.39 = (bf16[8,64,704]{2,1,0:T(8,128)(2,1)S(1)}, bf16[8,64,704]{2,1,0:T(8,128)(2,1)S(1)}, u32[]{:S(2)}, u32[]{:S(2)}) collective-permute-start(bf16[8,64,704]{2,1,0:T(8,128)(2,1)S(1)} %get-tuple-element.339), channel_id=1, source_target_pairs={{0,4},{4,0},{8,12},{12,8},{16,20},{20,16},{24,28},{28,24},{1,5},{5... | collective-permute-start | bytes 2162696 | tf_op jit(solution)/shard_map/ppermute | solution.py:31
  196.1 19.6 %collective-permute-start.40 = (bf16[8,64,704]{2,1,0:T(8,128)(2,1)S(1)}, bf16[8,64,704]{2,1,0:T(8,128)(2,1)S(1)}, u32[]{:S(2)}, u32[]{:S(2)}) collective-permute-start(bf16[8,64,704]{2,1,0:T(8,128)(2,1)S(1)} %get-tuple-element.340), channel_id=1, source_target_pairs={{0,2},{1,3},{2,0},{3,1},{4,6},{5,7},{6,4},{7,5},{8,10},{9,11},{10,... | collective-permute-start | bytes 2162696 | tf_op jit(solution)/shard_map/ppermute | solution.py:31
  239.9 18.9 %collective-permute-start.46 = (bf16[8,64,768]{2,1,0:T(8,128)(2,1)S(1)}, bf16[8,64,768]{2,1,0:T(8,128)(2,1)S(1)}, u32[]{:S(2)}, u32[]{:S(2)}) collective-permute-start(bf16[8,64,768]{2,1,0:T(8,128)(2,1)S(1)} %pad_maximum_fusion.15), channel_id=1, source_target_pairs={{0,2},{1,3},{2,0},{3,1},{4,6},{5,7},{6,4},{7,5},{8,10},{9,11},{10,... | collective-permute-start | bytes 2359304 | tf_op jit(solution)/shard_map/ppermute | solution.py:31
  240.3 18.5 %collective-permute-start.47 = (bf16[2,2,88,1024]{3,2,1,0:T(8,128)(2,1)S(1)}, bf16[2,2,88,1024]{3,2,1,0:T(8,128)(2,1)S(1)}, u32[]{:S(2)}, u32[]{:S(2)}) collective-permute-start(bf16[2,2,88,1024]{3,2,1,0:T(8,128)(2,1)S(1)} %get-tuple-element.395), channel_id=1, source_target_pairs={{0,4},{4,0},{8,12},{12,8},{16,20},{20,16},{24,28},{28,24},{1,5},{5... | collective-permute-start | bytes 2162696 | tf_op jit(solution)/shard_map/ppermute | solution.py:31
  242.0 16.8 %collective-permute-start.48 = (bf16[64,1408]{1,0:T(8,128)(2,1)S(1)}, bf16[64,1408]{1,0:T(8,128)(2,1)S(1)}, u32[]{:S(2)}, u32[]{:S(2)}) collective-permute-start(bf16[64,1408]{1,0:T(8,128)(2,1)S(1)} %get-tuple-element.401), channel_id=1, source_target_pairs={{0,8},{4,12},{8,0},{12,4},{16,24},{20,28},{24,16},{28,20},{1,9},{5... | collective-permute-start | bytes 540680 | tf_op jit(solution)/shard_map/ppermute | solution.py:31
  281.0 18.9 %collective-permute-start.60 = (bf16[192,1024]{1,0:T(8,128)(2,1)}, bf16[192,1024]{1,0:T(8,128)(2,1)S(1)}, u32[]{:S(2)}, u32[]{:S(2)}) collective-permute-start(bf16[192,1024]{1,0:T(8,128)(2,1)} %get-tuple-element.446), channel_id=1, source_target_pairs={{0,8},{4,12},{8,0},{12,4},{16,24},{20,28},{24,16},{28,20},{1,9},{5... | collective-permute-start | bytes 1179656 | tf_op jit(solution)/shard_map/ppermute | solution.py:31
  283.1 23.6 %collective-permute-start.57 = (bf16[160,1024]{1,0:T(8,128)(2,1)}, bf16[160,1024]{1,0:T(8,128)(2,1)S(1)}, u32[]{:S(2)}, u32[]{:S(2)}) collective-permute-start(bf16[160,1024]{1,0:T(8,128)(2,1)} %get-tuple-element.441), channel_id=1, source_target_pairs={{0,16},{4,20},{8,24},{12,28},{16,0},{20,4},{24,8},{28,12},{1,17},{... | collective-permute-start | bytes 983048 | tf_op jit(solution)/shard_map/ppermute | solution.py:31
  283.3 19.6 %collective-permute-start.56 = (bf16[64,1024]{1,0:T(8,128)(2,1)}, bf16[64,1024]{1,0:T(8,128)(2,1)}, u32[]{:S(2)}, u32[]{:S(2)}) collective-permute-start(bf16[64,1024]{1,0:T(8,128)(2,1)} %copy-done.76), channel_id=1, source_target_pairs={{0,8},{4,12},{8,0},{12,4},{16,24},{20,28},{24,16},{28,20},{1,9},{5... | collective-permute-start | bytes 393224 | tf_op jit(solution)/shard_map/ppermute | solution.py:31
  285.2 21.6 %collective-permute-start.58 = (bf16[64,1024]{1,0:T(8,128)(2,1)}, bf16[64,1024]{1,0:T(8,128)(2,1)}, u32[]{:S(2)}, u32[]{:S(2)}) collective-permute-start(bf16[64,1024]{1,0:T(8,128)(2,1)} %copy-done.75), channel_id=1, source_target_pairs={{0,24},{4,28},{8,16},{12,20},{16,8},{20,12},{24,0},{28,4},{1,25},{... | collective-permute-start | bytes 393224 | tf_op jit(solution)/shard_map/ppermute | solution.py:31
  (140 other events, 1269.8 us)
